TPU v7x, 32 devices: a whole 2x2x4 slice. The times are simulated.
32 devices in a mesh: row: 8 (over z, x), col: 4 (over y, core).
Axes of the slice: x: 2, y: 2, z: 4, core: 2. Of those that a mesh axis runs over, the one named last changes fastest.
Arguments:
- incident: float32 [2, 36, 8192], P(None, None, 'row'), may hold values from -24 to 24
- diagonal: float32 [8192], P('row'), may hold values from 1 to 2
- near_blocks: bfloat16 [8, 8, 2, 1024, 1024], P('row', None, None, None, 'col'), may hold values from -0.046875 to 0.046875
- left_factors: bfloat16 [8, 8, 2, 64, 1024], P('row', 'col'), may hold values from -0.0390625 to 0.0390625
- right_factors: bfloat16 [8, 8, 2, 64, 1024], P('row', 'col'), may hold values from -0.1875 to 0.1875
- flags: int32 [8, 8], P('row'), may hold values from 0 to 1, as said below
- ranks: int32 [8, 8], P('row', 'col'), may hold values from 4 to 64
- harmonics: float32 [2, 36, 8192], P(None, None, 'row'), may hold values from -0.0625 to 0.0625
Outputs:
- solution: float32 [2, 36, 8192], P(None, None, 'row')
- coefficients: float32 [2, 36, 36], replicated
Inputs may be any that keep to these rules, and one draw needn't show every extreme that they name: `flags`: slot 8 / 2 (the pair of a cluster with itself) is always 1; the ones of a row form one run of slots around it.
All inputs are finite; a program needn't handle non-finite values.
Results may differ from a plain program's by a relative error of at most 0.0013.
Values may be sent and summed in bfloat16 or wider, within the bound.
No kernel may reach another device: no remote copies, remote signals or barrier semaphores. Data moves between devices by JAX's collectives and lax.ppermute only.
A program may use at most 128 MiB of HBM per device.

v0:
```python
import functools

import jax
import jax.numpy as jnp
from jax import lax
from jax.experimental import pallas as pl
from jax.experimental.pallas import tpu as pltpu
from jax.sharding import PartitionSpec as P

F32 = jnp.float32
BF16 = jnp.bfloat16
SHIFT = 1.5
highest = lax.Precision.HIGHEST
MIB = 1024 * 1024


def dot_t(left, right, precision=None):
    return lax.dot_general(
        left, right, (((1,), (1,)), ((), ())), precision=precision, preferred_element_type=F32
    )


def dot_n(left, right, precision=highest):
    return lax.dot_general(
        left, right, (((1,), (0,)), ((), ())), precision=precision, preferred_element_type=F32
    )


def split(a):
    high = a.astype(BF16)
    return high, (a - high.astype(F32)).astype(BF16)


def dot_split(left, right, dot):
    (lh, ll), (rh, rl) = split(left), split(right)
    return dot(lh, rh, None) + (dot(lh, rl, None) + dot(ll, rh, None))


def near_kernel(rows, flags, v_ref, blocks_ref, out_ref, held, first, second, sems):
    slots = held.shape[0]
    half = out_ref.shape[0] // 2

    def fetch(k, part):
        return pltpu.make_async_copy(
            blocks_ref.at[0, k, part], held.at[k, part], sems.at[k, part]
        )

    for k in range(slots):
        for part in range(2):
            fetch(k, part).start()
    for k in range(slots):
        v = v_ref[(lax.axis_index("row") + k - slots // 2 + rows) % rows]
        v = jnp.where(flags[:, k : k + 1] == 1, v.astype(F32), 0.0).astype(BF16)
        for part in range(2):
            fetch(k, part).wait()
        for part, total in enumerate((first, second)):
            term = dot_t(v, held[k, part])
            if k == 0:
                total[...] = term
            else:
                total[...] += term
    fields = v_ref.shape[1] // 2
    out_ref[...] = jnp.zeros_like(out_ref)
    out_ref[:fields] = first[:fields] - second[fields:]
    out_ref[half : half + fields] = first[fields:] + second[:fields]


def near(flags, v, blocks, both):
    rows, twice, _ = v.shape
    _, slots, _, elements, width = blocks.shape
    return pl.pallas_call(
        functools.partial(near_kernel, rows),
        in_specs=[
            pl.BlockSpec(memory_space=pltpu.VMEM),
            pl.BlockSpec(memory_space=pltpu.VMEM),
            pl.BlockSpec(memory_space=pltpu.HBM),
        ],
        out_specs=pl.BlockSpec(memory_space=pltpu.VMEM),
        out_shape=jax.ShapeDtypeStruct((both, elements), F32),
        scratch_shapes=[
            pltpu.VMEM((slots, 2, elements, width), BF16),
            pltpu.VMEM((twice, elements), F32),
            pltpu.VMEM((twice, elements), F32),
            pltpu.SemaphoreType.DMA((slots, 2)),
        ],
        compiler_params=pltpu.CompilerParams(vmem_limit_bytes=53 * MIB),
        name="near",
    )(flags, v, blocks)


def far_kernel(rows, flags, ranks, v_ref, right_ref, left_ref, near_ref, out_ref):
    cols, both, width = out_ref.shape
    half = both // 2
    fields = v_ref.shape[2] // 2
    blocks, both_ranks, _ = right_ref.shape
    slots = flags.shape[1]
    rank = both_ranks // 2
    column = lax.axis_index("col")
    lane = lax.broadcasted_iota(jnp.int32, (half, both_ranks), 1)
    low = lane < rank

    def used(b):
        slot = (column * blocks + b - lax.axis_index("row") + slots // 2 + rows) % rows
        here = lax.broadcasted_iota(jnp.int32, (1, slots), 1) == slot
        is_near = jnp.max(jnp.where(here & (flags[...] == 1), 1, 0), axis=1, keepdims=True)
        return ranks[:, b : b + 1] * (1 - is_near)

    upper, lower = [], []
    for b in range(blocks):
        t = jnp.zeros((2 * fields, both_ranks), F32)
        for s in range(cols):
            part = pl.ds(pl.multiple_of(jnp.bitwise_xor(column, s) * width, width), width)
            t = t + dot_t(v_ref[s, b], right_ref[b, :, part])
        gap = jnp.zeros((half - fields, both_ranks), F32)
        real = jnp.concatenate([t[:fields], gap], axis=0)
        turned = jnp.concatenate([pltpu.roll(t, rank, 1)[fields:], gap], axis=0)
        z = jnp.where(low, real - turned, real + turned)
        z = jnp.where(lax.rem(lane, rank) < used(b), z, 0.0)
        upper.append(jnp.where(low, z, -z))
        lower.append(pltpu.roll(z, rank, 1))
    mixed = jnp.concatenate(
        [jnp.concatenate(upper, axis=1), jnp.concatenate(lower, axis=1)], axis=0
    ).astype(BF16)
    for q in range(cols):
        place = jnp.bitwise_xor(column, q)
        part = slice(q * width, (q + 1) * width)
        out_ref[place] = near_ref[:, part] + dot_n(mixed, left_ref[:, part], None)


def gram_one_kernel(shift, b_ref, p_ref, h_ref, out_ref):
    both = b_ref.shape[0]
    half = both // 2
    b, p, h = b_ref[...], p_ref[...], h_ref[...]
    ab = p + shift * b
    grams = jnp.zeros((2 * half, half), F32)
    for part in range(2):
        rows = slice(part * half, (part + 1) * half)
        grams += dot_split(jnp.concatenate([ab[rows], b[rows]], axis=0), ab[rows], dot_t)
    shots = dot_split(h, jnp.concatenate([b, p], axis=0), dot_t)
    pieces = [grams[:half], grams[half:]]
    for n in range(2):
        q = shots[:, n * both : (n + 1) * both]
        pieces.append(q[:half, :half] + q[half:, half:])
        pieces.append(q[:half, half:] - q[half:, :half])
    out_ref[...] = jnp.concatenate(pieces, axis=1)


def gram_two_kernel(shift, b_ref, p_ref, a_ref, out_ref):
    slots, both, _ = b_ref.shape
    half = both // 2
    total = jnp.zeros((half, 3 * half), F32)
    for n in range(slots):
        s = jnp.bitwise_xor(lax.axis_index("col") // 2, n)
        for part in range(2):
            rows = slice(part * half, (part + 1) * half)
            b, p, a = b_ref[s, rows], p_ref[s, rows], a_ref[s, rows]
            total += dot_split(a, jnp.concatenate([a, p + shift * b, b], axis=0), dot_t)
    out_ref[...] = total


def eliminate(m, size):
    index = lax.broadcasted_iota(jnp.int32, m.shape, 0)
    column = jnp.broadcast_to(m[:, :1], m.shape)
    for k in range(size):
        ahead = jnp.broadcast_to(m[:, k + 1 : k + 2], m.shape)
        scale = 1.0 / column[k : k + 1]
        row = m[k : k + 1] * scale
        first = ahead[k : k + 1] * scale
        m = jnp.where(index == k, row, m - column * row)
        column = jnp.where(index == k, first, ahead - column * first)
    return m


def unit_padding(size, fields):
    r = lax.broadcasted_iota(jnp.int32, (size, size), 0)
    c = lax.broadcasted_iota(jnp.int32, (size, size), 1)
    return jnp.where((r == c) & (r >= fields), 1.0, 0.0)


def invert_kernel(fields, g1_ref, out_ref):
    half = g1_ref.shape[0]
    pad = unit_padding(half, fields)
    r = lax.broadcasted_iota(jnp.int32, (half, half), 0)
    c = lax.broadcasted_iota(jnp.int32, (half, half), 1)
    eye = jnp.where(r == c, 1.0, 0.0)
    m = jnp.concatenate([g1_ref[:, :half] + pad, eye, g1_ref[:, half : 2 * half].T], axis=1)
    m = eliminate(m, fields)
    out_ref[...] = m[:, half:]


def solve_kernel(fields, inv_ref, g1_ref, g2_ref, b_ref, p_ref, x_ref, c_ref):
    half = inv_ref.shape[0]
    cols, both, width = p_ref.shape
    g2 = g2_ref[0]
    for n in range(1, g2_ref.shape[0]):
        g2 = g2 + g2_ref[n]
    z22 = g2[:, :half] + unit_padding(half, fields)
    z21 = g2[:, half : 2 * half]
    z2b = g2[:, 2 * half : 3 * half]
    inv = inv_ref[:, :half]
    w1b = inv_ref[:, half:]
    mixed = dot_t(inv, z21, highest)
    step = dot_n(z21, jnp.concatenate([mixed, w1b], axis=1))
    m = eliminate(jnp.concatenate([z22, z2b], axis=1) - step, fields)
    w2 = m[:, half:]
    w1 = w1b - dot_n(mixed, w2)
    y1 = w1.T
    y2 = w2.T
    for n in range(2):
        hb = g1_ref[:, (2 + n) * half : (3 + n) * half]
        hp = g1_ref[:, (4 + n) * half : (5 + n) * half]
        total = dot_t(hb, y1, highest) + dot_t(hp, y2, highest)
        c_ref[:, n, :] = total[: c_ref.shape[0], :fields]
    y = jnp.concatenate([y1, y2], axis=1)
    for q in range(cols):
        place = jnp.bitwise_xor(lax.axis_index("col"), q)
        for part in range(2):
            rows = slice(part * half, (part + 1) * half)
            basis = jnp.concatenate([b_ref[place, rows], p_ref[place, rows]], axis=0)
            x = dot_split(y, basis, dot_n)
            x_ref[:, part, q * width : (q + 1) * width] = x[:fields]


def whole_call(kernel, out_shape, name, *args, cost=None):
    vmem = pl.BlockSpec(memory_space=pltpu.VMEM)
    single = not isinstance(out_shape, (list, tuple))
    return pl.pallas_call(
        kernel,
        in_specs=[vmem] * len(args),
        out_specs=vmem if single else [vmem] * len(out_shape),
        out_shape=out_shape,
        cost_estimate=cost,
        compiler_params=pltpu.CompilerParams(vmem_limit_bytes=12 * MIB),
        name=name,
    )(*args)


def swap(array, axis, bit):
    size = lax.axis_size(axis)
    return lax.ppermute(array, axis, [(n, n ^ bit) for n in range(size)])


def spread(array, axis):
    size = lax.axis_size(axis)
    copies = jnp.broadcast_to(array[None], (size,) + array.shape)
    return lax.all_to_all(copies, axis, 0, 0)


def spread_start(array, axis):
    size = lax.axis_size(axis)
    return jnp.broadcast_to(array[None], (size,) + array.shape)


def body(incident, diagonal, near_blocks, left_factors, right_factors, flags, ranks, harmonics):
    _, blocks, _, rank, elements = left_factors.shape
    slots, width = near_blocks.shape[1], near_blocks.shape[4]
    fields = incident.shape[1]
    cols, rows = lax.axis_size("col"), lax.axis_size("row")
    column = lax.axis_index("col")
    half = -(-fields // 8) * 8
    bits = [1 << n for n in range(cols.bit_length() - 1)]
    row_bits = [1 << n for n in range(rows.bit_length() - 1)]

    def place(s):
        return jnp.bitwise_xor(column, s) * width

    def cut(array, s):
        piece = lax.dynamic_slice_in_dim(array, place(s), width, 2)
        piece = jnp.pad(piece, ((0, 0), (0, half - array.shape[1]), (0, 0)))
        return piece.reshape(2 * half, width)

    def sent(array):
        array = array.astype(BF16)
        return jnp.concatenate([array[:fields], array[half : half + fields]], axis=0)

    b_first = cut(incident, 0)
    copies = spread_start(sent(b_first), "row")
    gathered = lax.all_to_all(copies, "row", 0, 0)
    rights = right_factors.reshape(blocks, 2 * rank, elements)
    lefts = left_factors.reshape(blocks * 2 * rank, elements)

    def operator(gathered, one=None):
        def piece(s):
            return lax.dynamic_slice_in_dim(
                gathered, jnp.bitwise_xor(column, s) * blocks, blocks, 0
            )

        pieces = [piece(0)] + [swap(piece(s), "col", s) for s in range(1, cols)]
        total = near(flags, gathered, near_blocks, 2 * half)
        if one is not None:
            total, one = lax.optimization_barrier((total, one + swap(one, "row", row_bits[-1])))
        total = whole_call(
            functools.partial(far_kernel, rows),
            jax.ShapeDtypeStruct((cols, 2 * half, width), F32),
            "far",
            flags,
            ranks,
            jnp.stack(pieces),
            rights,
            lefts,
            total,
        )
        return total if one is None else (total, one)

    total = operator(gathered)
    total = total[0::2] + swap(total[1::2], "col", 1)
    for bit in reversed(bits[1:]):
        n = total.shape[0] // 2
        total = total[:n] + swap(total[n:], "col", bit)
    d_first = lax.dynamic_slice_in_dim(diagonal, place(0), width, 0)
    p_first = total[0] + (d_first - SHIFT)[None, :] * b_first

    copies = spread_start(sent(p_first), "row")
    copies, p_early = lax.optimization_barrier((copies, p_first))
    gathered = lax.all_to_all(copies, "row", 0, 0)

    one = whole_call(
        functools.partial(gram_one_kernel, SHIFT),
        jax.ShapeDtypeStruct((half, 6 * half), F32),
        "gram_one",
        b_first,
        p_early,
        cut(harmonics, 0),
    )
    for bit in bits:
        one = one + swap(one, "col", bit)
    b_all = jnp.stack([b_first] + [cut(incident, s) for s in range(1, cols)])
    b_own = b_all[0::2]
    p_own = p_early[None]
    for bit in bits[1:]:
        p_own = jnp.concatenate([p_own, swap(p_own, "col", bit)])
    gathered, one, p_own = lax.optimization_barrier((gathered, one, p_own))
    p_all = jnp.stack([p_own, swap(p_own, "col", 1)], axis=1).reshape(cols, 2 * half, width)

    total, one = operator(gathered, one)
    for bit in reversed(row_bits[1:-1]):
        one = one + swap(one, "row", bit)
    total = (total[0::2] + swap(total[1::2], "col", 1)).astype(BF16)
    for bit in bits[1:]:
        other = swap(total, "col", bit).astype(F32)
        total = total.astype(F32) + jnp.stack([other[s ^ (bit // 2)] for s in range(cols // 2)])
        total = total if bit == bits[-1] else total.astype(BF16)
    d_own = jnp.stack(
        [lax.dynamic_slice_in_dim(diagonal, place(s), width, 0) for s in range(0, cols, 2)]
    )
    ap, one = lax.optimization_barrier((total + d_own[:, None, :] * p_own, one))
    one = one + swap(one, "row", row_bits[0])
    two = whole_call(
        functools.partial(gram_two_kernel, SHIFT),
        jax.ShapeDtypeStruct((half, 3 * half), F32),
        "gram_two",
        b_own,
        p_own,
        ap,
    )
    two = spread(two + swap(two, "col", 1), "row")
    inverse = whole_call(
        functools.partial(invert_kernel, fields),
        jax.ShapeDtypeStruct((half, 2 * half), F32),
        "invert",
        one,
    )
    return tuple(
        array.transpose(1, 0, 2)
        for array in whole_call(
            functools.partial(solve_kernel, fields),
            [
                jax.ShapeDtypeStruct((fields, 2, elements), F32),
                jax.ShapeDtypeStruct((harmonics.shape[1], 2, fields), F32),
            ],
            "solve",
            inverse,
            one,
            two,
            b_all,
            p_all,
        )
    )


def solution(mesh):
    in_specs = (
        P(None, None, "row"),
        P("row"),
        P("row", None, None, None, "col"),
        P("row", "col", None, None, None),
        P("row", "col", None, None, None),
        P("row", None),
        P("row", "col"),
        P(None, None, "row"),
    )
    out_specs = (P(None, None, "row"), P())
    return jax.shard_map(body, mesh=mesh, in_specs=in_specs, out_specs=out_specs, check_vma=False)
```

profile of v0, /device:TPU:0, one launch (start us, length us, event | category | flops | bytes accessed | tf_op | source)
XLA Modules:
  0.0 79.2 jit_solution(1964547995468984332)
XLA Ops:
  0.6 0.0 copy-start.4
  0.6 0.0 copy-start
  0.7 0.0 copy-start.1
  0.7 0.0 copy-start.5
  0.7 1.3 %constant_dynamic-slice_fusion.2 = (f32[2,36,256]{2,0,1:T(2,128)S(1)}, f32[2,36,256]{2,0,1:T(2,128)S(1)}, f32[2,36,256]{2,0,1:T(2,128)S(1)}, f32[2,36,256]{2,0,1:T(2,128)S(1)}, f32[2,36,256]{2,0,1:T(2,128)S(1)}) fusion(f32[2,36,1024]{2,0,1:T(2,128)} %param.8, s32[]{:T(128)S(6)} %select_n.38, s32[]{:T(128)S(6)} %select_n.32, s32[]{:T(128)S(6)} %select_n.39, ...), kind=kLoop, calls=%fused_computation.18 | loop fusion | bytes 737296 | tf_op jit(solution)/shard_map/dynamic_slice | solution.py:268
  2.0 0.7 broadcast_in_dim.8
  2.8 7.4 %all-to-all-start = ((bf16[8,72,256]{2,1,0:T(8,128)(2,1)}), bf16[8,72,256]{2,1,0:T(8,128)(2,1)S(1)}, u32[]{:S(2)}, u32[]{:S(2)}) async-start(bf16[8,72,256]{2,1,0:T(8,128)(2,1)} %broadcast_in_dim.8), calls=%async_computation | async-start | bytes 589824 | tf_op jit(solution)/shard_map/all_to_all | solution.py:278
  10.1 9.6 %all-to-all-done.v_ref = bf16[8,72,256]{2,1,0:T(8,128)(2,1)S(1)} async-done(((bf16[8,72,256]{2,1,0:T(8,128)(2,1)}), bf16[8,72,256]{2,1,0:T(8,128)(2,1)S(1)}, u32[]{:S(2)}, u32[]{:S(2)}) %all-to-all-start) | async-done | bytes 294944 | tf_op jit(solution)/shard_map/all_to_all | solution.py:278
  19.8 0.1 collective-permute-start.2
  19.9 1.6 %collective-permute-start.1 = (bf16[2,72,256]{2,1,0:T(8,128)(2,1)S(1)}, bf16[2,72,256]{2,1,0:T(8,128)(2,1)S(1)}, u32[]{:S(2)}, u32[]{:S(2)}) collective-permute-start(bf16[2,72,256]{2,1,0:T(8,128)(2,1)S(1)} %get-tuple-element.38), channel_id=1, source_target_pairs={{0,2},{1,3},{2,0},{3,1},{4,6},{5,7},{6,4},{7,5},{8,10},{9,11},{10,... | collective-permute-start | bytes 221192 | tf_op jit(solution)/shard_map/ppermute | solution.py:240
  21.5 0.3 collective-permute-start
  21.7 0.7 copy-done.2
  22.4 4.1 %near.2.near_ref = f32[80,1024]{1,0:T(8,128)S(1)} custom-call(s32[1,8]{1,0:T(1,128)S(1)} %copy-done.2, bf16[8,72,256]{2,1,0:T(8,128)(2,1)S(1)} %all-to-all-done.v_ref, bf16[1,8,2,1024,256]{4,3,2,1,0:T(8,128)(2,1)} %blocks_ref.3), custom_call_target="tpu_custom_call" | custom-call | tf_op jit(solution)/shard_map/near/pallas_call | solution.py:71
  26.5 0.0 collective-permute-done.2
  26.5 0.0 collective-permute-done.1
  26.5 0.0 collective-permute-done
  26.6 0.0 copy-done.4
  26.6 0.0 copy-done
  26.6 0.6 far.2
  27.3 0.3 collective-permute-start.3
  27.6 1.1 %collective-permute-done.3 = f32[2,80,256]{2,1,0:T(8,128)S(1)} collective-permute-done((f32[2,80,256]{2,1,0:T(8,128)S(1)}, f32[2,80,256]{2,1,0:T(8,128)S(1)}, u32[]{:S(2)}, u32[]{:S(2)}) %collective-permute-start.3) | collective-permute-done | bytes 163872 | tf_op jit(solution)/shard_map/ppermute | solution.py:240
  28.8 1.6 %collective-permute-start.4 = (f32[1,80,256]{2,1,0:T(8,128)S(1)}, f32[1,80,256]{2,1,0:T(8,128)S(1)}, u32[]{:S(2)}, u32[]{:S(2)}) collective-permute-start(f32[1,80,256]{2,1,0:T(8,128)S(1)} %slice.55), channel_id=1, source_target_pairs={{0,2},{1,3},{2,0},{3,1},{4,6},{5,7},{6,4},{7,5},{8,10},{9,11},{10,... | collective-permute-start | bytes 245768 | tf_op jit(solution)/shard_map/ppermute | solution.py:240
  30.3 0.0 copy-done.5
  30.4 0.1 broadcast_add_fusion
  30.4 3.0 %collective-permute-done.4 = f32[1,80,256]{2,1,0:T(8,128)S(1)} collective-permute-done((f32[1,80,256]{2,1,0:T(8,128)S(1)}, f32[1,80,256]{2,1,0:T(8,128)S(1)}, u32[]{:S(2)}, u32[]{:S(2)}) %collective-permute-start.4) | collective-permute-done | bytes 81952 | tf_op jit(solution)/shard_map/ppermute | solution.py:240
  33.5 0.7 broadcast_in_dim.9
  34.2 3.6 %all-to-all-start.1 = ((bf16[8,72,256]{2,1,0:T(8,128)(2,1)}), bf16[8,72,256]{2,1,0:T(8,128)(2,1)S(1)}, u32[]{:S(2)}, u32[]{:S(2)}) async-start(bf16[8,72,256]{2,1,0:T(8,128)(2,1)} %broadcast_in_dim.9), calls=%async_computation.1 | async-start | bytes 589824 | tf_op jit(solution)/shard_map/all_to_all | solution.py:315
  37.8 1.4 %collective-permute-start.7 = (f32[1,80,256]{2,1,0:T(8,128)S(1)}, f32[1,80,256]{2,1,0:T(8,128)S(1)}, u32[]{:S(2)}, u32[]{:S(2)}) collective-permute-start(f32[1,80,256]{2,1,0:T(8,128)S(1)} %bitcast.42), channel_id=1, source_target_pairs={{0,2},{1,3},{2,0},{3,1},{4,6},{5,7},{6,4},{7,5},{8,10},{9,11},{10,... | collective-permute-start | bytes 245768 | tf_op jit(solution)/shard_map/ppermute | solution.py:240
  39.2 0.4 gram_one.1
  39.7 0.1 collective-permute-start.5
  39.7 1.2 %collective-permute-done.5 = f32[40,240]{1,0:T(8,128)S(1)} collective-permute-done((f32[40,240]{1,0:T(8,128)S(1)}, f32[40,240]{1,0:T(8,128)S(1)}, u32[]{:S(2)}, u32[]{:S(2)}) %collective-permute-start.5) | collective-permute-done | bytes 38432 | tf_op jit(solution)/shard_map/ppermute | solution.py:240
  41.0 0.6 collective-permute-start.6
  41.6 3.4 %collective-permute-done.6 = f32[40,240]{1,0:T(8,128)S(1)} collective-permute-done((f32[40,240]{1,0:T(8,128)S(1)}, f32[40,240]{1,0:T(8,128)S(1)}, u32[]{:S(2)}, u32[]{:S(2)}) %collective-permute-start.6) | collective-permute-done | bytes 38432 | tf_op jit(solution)/shard_map/ppermute | solution.py:240
  45.0 0.0 collective-permute-done.7
  45.0 2.0 %all-to-all-done.1.v_ref = bf16[8,72,256]{2,1,0:T(8,128)(2,1)S(1)} async-done(((bf16[8,72,256]{2,1,0:T(8,128)(2,1)}), bf16[8,72,256]{2,1,0:T(8,128)(2,1)S(1)}, u32[]{:S(2)}, u32[]{:S(2)}) %all-to-all-start.1) | async-done | bytes 294944 | tf_op jit(solution)/shard_map/all_to_all | solution.py:315
  47.0 0.1 collective-permute-start.10
  47.1 1.4 %collective-permute-start.9 = (bf16[2,72,256]{2,1,0:T(8,128)(2,1)S(1)}, bf16[2,72,256]{2,1,0:T(8,128)(2,1)S(1)}, u32[]{:S(2)}, u32[]{:S(2)}) collective-permute-start(bf16[2,72,256]{2,1,0:T(8,128)(2,1)S(1)} %get-tuple-element.34), channel_id=1, source_target_pairs={{0,2},{1,3},{2,0},{3,1},{4,6},{5,7},{6,4},{7,5},{8,10},{9,11},{10,... | collective-permute-start | bytes 221192 | tf_op jit(solution)/shard_map/ppermute | solution.py:240
  48.5 0.5 collective-permute-start.8
  49.0 1.0 %collective-permute-start.11 = (f32[40,240]{1,0:T(8,128)S(1)}, f32[40,240]{1,0:T(8,128)S(1)}, u32[]{:S(2)}, u32[]{:S(2)}) collective-permute-start(f32[40,240]{1,0:T(8,128)S(1)} %add.88), channel_id=1, source_target_pairs={{0,16},{4,20},{8,24},{12,28},{16,0},{20,4},{24,8},{28,12},{1,17},{... | collective-permute-start | bytes 115208 | tf_op jit(solution)/shard_map/ppermute | solution.py:240
  50.0 0.0 copy-done.3
  50.0 4.1 %near.3.near_ref = f32[80,1024]{1,0:T(8,128)S(1)} custom-call(s32[1,8]{1,0:T(1,128)S(1)} %copy-done.3, bf16[8,72,256]{2,1,0:T(8,128)(2,1)S(1)} %all-to-all-done.1.v_ref, bf16[1,8,2,1024,256]{4,3,2,1,0:T(8,128)(2,1)} %blocks_ref.3), custom_call_target="tpu_custom_call" | custom-call | tf_op jit(solution)/shard_map/near/pallas_call | solution.py:71
  54.2 0.0 collective-permute-done.11
  54.2 0.0 collective-permute-done.10
  54.2 0.0 collective-permute-done.9
  54.2 0.0 collective-permute-done.8
  54.3 0.6 far.3
  54.9 0.1 collective-permute-start.12
  55.1 1.4 %collective-permute-start.14 = (f32[40,240]{1,0:T(8,128)S(1)}, f32[40,240]{1,0:T(8,128)S(1)}, u32[]{:S(2)}, u32[]{:S(2)}) collective-permute-start(f32[40,240]{1,0:T(8,128)S(1)} %add.89), channel_id=1, source_target_pairs={{0,8},{4,12},{8,0},{12,4},{16,24},{20,28},{24,16},{28,20},{1,9},{5... | collective-permute-start | bytes 115208 | tf_op jit(solution)/shard_map/ppermute | solution.py:240
  56.5 0.0 collective-permute-done.12
  56.6 1.2 %collective-permute-start.13 = (bf16[2,80,256]{2,1,0:T(8,128)(2,1)S(1)}, bf16[2,80,256]{2,1,0:T(8,128)(2,1)S(1)}, u32[]{:S(2)}, u32[]{:S(2)}) collective-permute-start(bf16[2,80,256]{2,1,0:T(8,128)(2,1)S(1)} %add_convert_fusion), channel_id=1, source_target_pairs={{0,2},{1,3},{2,0},{3,1},{4,6},{5,7},{6,4},{7,5},{8,10},{9,11},{10,... | collective-permute-start | bytes 245768 | tf_op jit(solution)/shard_map/ppermute | solution.py:240
  57.8 1.4 %collective-permute-done.14 = f32[40,240]{1,0:T(8,128)S(1)} collective-permute-done((f32[40,240]{1,0:T(8,128)S(1)}, f32[40,240]{1,0:T(8,128)S(1)}, u32[]{:S(2)}, u32[]{:S(2)}) %collective-permute-start.14) | collective-permute-done | bytes 38432 | tf_op jit(solution)/shard_map/ppermute | solution.py:240
  59.2 2.0 %collective-permute-done.13 = bf16[2,80,256]{2,1,0:T(8,128)(2,1)S(1)} collective-permute-done((bf16[2,80,256]{2,1,0:T(8,128)(2,1)S(1)}, bf16[2,80,256]{2,1,0:T(8,128)(2,1)S(1)}, u32[]{:S(2)}, u32[]{:S(2)}) %collective-permute-start.13) | collective-permute-done | bytes 81952 | tf_op jit(solution)/shard_map/ppermute | solution.py:240
  61.2 0.4 gram_two.1
  61.6 0.1 collective-permute-start.16
  61.7 0.5 collective-permute-start.17
  62.2 0.7 collective-permute-done.16
  62.9 0.7 broadcast_in_dim.11
  63.5 4.2 %all-to-all-start.2 = ((f32[8,40,120]{2,1,0:T(8,128)}), f32[8,40,120]{2,1,0:T(8,128)S(1)}, u32[]{:S(2)}, u32[]{:S(2)}) async-start(f32[8,40,120]{2,1,0:T(8,128)} %broadcast_in_dim.11), calls=%async_computation.2 | async-start | bytes 327680 | tf_op jit(solution)/shard_map/all_to_all | solution.py:246
  67.7 2.0 %collective-permute-start.15 = (f32[40,240]{1,0:T(8,128)S(1)}, f32[40,240]{1,0:T(8,128)S(1)}, u32[]{:S(2)}, u32[]{:S(2)}) collective-permute-start(f32[40,240]{1,0:T(8,128)S(1)} %add.94), channel_id=1, source_target_pairs={{0,4},{4,0},{8,12},{12,8},{16,20},{20,16},{24,28},{28,24},{1,5},{5... | collective-permute-start | bytes 115208 | tf_op jit(solution)/shard_map/ppermute | solution.py:240
  69.7 0.0 collective-permute-done.17
  69.8 2.8 %collective-permute-done.15 = f32[40,240]{1,0:T(8,128)S(1)} collective-permute-done((f32[40,240]{1,0:T(8,128)S(1)}, f32[40,240]{1,0:T(8,128)S(1)}, u32[]{:S(2)}, u32[]{:S(2)}) %collective-permute-start.15) | collective-permute-done | bytes 38432 | tf_op jit(solution)/shard_map/ppermute | solution.py:240
  72.6 1.9 %invert.1.inv_ref = f32[40,80]{1,0:T(8,128)S(1)} custom-call(f32[40,240]{1,0:T(8,128)S(1)} %add.95.g1_ref), custom_call_target="tpu_custom_call" | custom-call | tf_op jit(solution)/shard_map/invert/pallas_call | solution.py:227
  74.5 1.0 %all-to-all-done.2.g2_ref = f32[8,40,120]{2,1,0:T(8,128)S(1)} async-done(((f32[8,40,120]{2,1,0:T(8,128)}), f32[8,40,120]{2,1,0:T(8,128)S(1)}, u32[]{:S(2)}, u32[]{:S(2)}) %all-to-all-start.2) | async-done | bytes 153632 | tf_op jit(solution)/shard_map/all_to_all | solution.py:246
  75.5 3.7 %solve.1 = (f32[36,2,1024]{2,1,0:T(2,128)}, f32[36,2,36]{2,1,0:T(2,128)}) custom-call(f32[40,80]{1,0:T(8,128)S(1)} %invert.1.inv_ref, f32[40,240]{1,0:T(8,128)S(1)} %add.95.g1_ref, f32[8,40,120]{2,1,0:T(8,128)S(1)} %all-to-all-done.2.g2_ref, f32[4,80,256]{2,1,0:T(8,128)S(1)} %pad_maximum_fusion.b_ref, f32[4,80,256]{2,1,0:T(8,128)S(1)} %bitcast.41), custom_call_target="tpu_custom_call" | custom-call | tf_op jit(solution)/shard_map/solve/pallas_call | solution.py:227
  (42 shorter events, 0.5 us)
Async XLA Ops:
  0.6 26.0 %copy-start.4 = (s32[1,2]{1,0:T(1,128)S(1)}, s32[1,2]{1,0:T(1,128)}, u32[]{:S(2)}) copy-start(s32[1,2]{1,0:T(1,128)} %ranks.3) | copy-start | bytes 28
  0.6 26.0 %copy-start = (bf16[1,2,2,64,1024]{4,3,2,1,0:T(8,128)(2,1)S(1)}, bf16[1,2,2,64,1024]{4,3,2,1,0:T(8,128)(2,1)}, u32[]{:S(2)}) copy-start(bf16[1,2,2,64,1024]{4,3,2,1,0:T(8,128)(2,1)} %param.12) | copy-start | bytes 1572868
  0.7 26.0 %copy-start.1 = (bf16[1,2,2,64,1024]{4,3,2,1,0:T(8,128)(2,1)S(1)}, bf16[1,2,2,64,1024]{4,3,2,1,0:T(8,128)(2,1)}, u32[]{:S(2)}) copy-start(bf16[1,2,2,64,1024]{4,3,2,1,0:T(8,128)(2,1)} %param.11) | copy-start | bytes 1572868
  0.7 29.7 %copy-start.5 = (f32[1024]{0:T(1024)S(1)}, f32[1024]{0:T(1024)}, u32[]{:S(2)}) copy-start(f32[1024]{0:T(1024)} %param.9) | copy-start | bytes 12292
  2.8 47.3 %copy-start.3 = (s32[1,8]{1,0:T(1,128)S(1)}, s32[1,8]{1,0:T(1,128)}, u32[]{:S(2)}) copy-start(s32[1,8]{1,0:T(1,128)} %flags.7) | copy-start | bytes 100
  2.8 17.0 %all-to-all-start = ((bf16[8,72,256]{2,1,0:T(8,128)(2,1)}), bf16[8,72,256]{2,1,0:T(8,128)(2,1)S(1)}, u32[]{:S(2)}, u32[]{:S(2)}) async-start(bf16[8,72,256]{2,1,0:T(8,128)(2,1)} %broadcast_in_dim.8), calls=%async_computation | async-start | bytes 589824 | tf_op jit(solution)/shard_map/all_to_all | solution.py:278
  19.8 6.7 %collective-permute-start.2 = (bf16[2,72,256]{2,1,0:T(8,128)(2,1)S(1)}, bf16[2,72,256]{2,1,0:T(8,128)(2,1)S(1)}, u32[]{:S(2)}, u32[]{:S(2)}) collective-permute-start(bf16[2,72,256]{2,1,0:T(8,128)(2,1)S(1)} %get-tuple-element.37), channel_id=1, source_target_pairs={{0,3},{1,2},{2,1},{3,0},{4,7},{5,6},{6,5},{7,4},{8,11},{9,10},{10,... | collective-permute-start | bytes 221192 | tf_op jit(solution)/shard_map/ppermute | solution.py:240
  19.9 6.6 %collective-permute-start.1 = (bf16[2,72,256]{2,1,0:T(8,128)(2,1)S(1)}, bf16[2,72,256]{2,1,0:T(8,128)(2,1)S(1)}, u32[]{:S(2)}, u32[]{:S(2)}) collective-permute-start(bf16[2,72,256]{2,1,0:T(8,128)(2,1)S(1)} %get-tuple-element.38), channel_id=1, source_target_pairs={{0,2},{1,3},{2,0},{3,1},{4,6},{5,7},{6,4},{7,5},{8,10},{9,11},{10,... | collective-permute-start | bytes 221192 | tf_op jit(solution)/shard_map/ppermute | solution.py:240
  21.5 5.1 %collective-permute-start = (bf16[2,72,256]{2,1,0:T(8,128)(2,1)S(1)}, bf16[2,72,256]{2,1,0:T(8,128)(2,1)S(1)}, u32[]{:S(2)}, u32[]{:S(2)}) collective-permute-start(bf16[2,72,256]{2,1,0:T(8,128)(2,1)S(1)} %get-tuple-element.39), channel_id=1, source_target_pairs={{0,1},{1,0},{2,3},{3,2},{4,5},{5,4},{6,7},{7,6},{8,9},{9,8},{10,11... | collective-permute-start | bytes 221192 | tf_op jit(solution)/shard_map/ppermute | solution.py:240
  21.7 0.7 copy-start.2
  27.3 1.5 %collective-permute-start.3 = (f32[2,80,256]{2,1,0:T(8,128)S(1)}, f32[2,80,256]{2,1,0:T(8,128)S(1)}, u32[]{:S(2)}, u32[]{:S(2)}) collective-permute-start(f32[2,80,256]{2,1,0:T(8,128)S(1)} %slice.42), channel_id=1, source_target_pairs={{0,1},{1,0},{2,3},{3,2},{4,5},{5,4},{6,7},{7,6},{8,9},{9,8},{10,11... | collective-permute-start | bytes 491528 | tf_op jit(solution)/shard_map/ppermute | solution.py:240
  28.8 4.7 %collective-permute-start.4 = (f32[1,80,256]{2,1,0:T(8,128)S(1)}, f32[1,80,256]{2,1,0:T(8,128)S(1)}, u32[]{:S(2)}, u32[]{:S(2)}) collective-permute-start(f32[1,80,256]{2,1,0:T(8,128)S(1)} %slice.55), channel_id=1, source_target_pairs={{0,2},{1,3},{2,0},{3,1},{4,6},{5,7},{6,4},{7,5},{8,10},{9,11},{10,... | collective-permute-start | bytes 245768 | tf_op jit(solution)/shard_map/ppermute | solution.py:240
  34.2 12.8 %all-to-all-start.1 = ((bf16[8,72,256]{2,1,0:T(8,128)(2,1)}), bf16[8,72,256]{2,1,0:T(8,128)(2,1)S(1)}, u32[]{:S(2)}, u32[]{:S(2)}) async-start(bf16[8,72,256]{2,1,0:T(8,128)(2,1)} %broadcast_in_dim.9), calls=%async_computation.1 | async-start | bytes 589824 | tf_op jit(solution)/shard_map/all_to_all | solution.py:315
  37.8 7.2 %collective-permute-start.7 = (f32[1,80,256]{2,1,0:T(8,128)S(1)}, f32[1,80,256]{2,1,0:T(8,128)S(1)}, u32[]{:S(2)}, u32[]{:S(2)}) collective-permute-start(f32[1,80,256]{2,1,0:T(8,128)S(1)} %bitcast.42), channel_id=1, source_target_pairs={{0,2},{1,3},{2,0},{3,1},{4,6},{5,7},{6,4},{7,5},{8,10},{9,11},{10,... | collective-permute-start | bytes 245768 | tf_op jit(solution)/shard_map/ppermute | solution.py:240
  39.7 1.3 %collective-permute-start.5 = (f32[40,240]{1,0:T(8,128)S(1)}, f32[40,240]{1,0:T(8,128)S(1)}, u32[]{:S(2)}, u32[]{:S(2)}) collective-permute-start(f32[40,240]{1,0:T(8,128)S(1)} %gram_one.1), channel_id=1, source_target_pairs={{0,1},{1,0},{2,3},{3,2},{4,5},{5,4},{6,7},{7,6},{8,9},{9,8},{10,11... | collective-permute-start | bytes 115208 | tf_op jit(solution)/shard_map/ppermute | solution.py:240
  41.0 4.0 %collective-permute-start.6 = (f32[40,240]{1,0:T(8,128)S(1)}, f32[40,240]{1,0:T(8,128)S(1)}, u32[]{:S(2)}, u32[]{:S(2)}) collective-permute-start(f32[40,240]{1,0:T(8,128)S(1)} %add.87), channel_id=1, source_target_pairs={{0,2},{1,3},{2,0},{3,1},{4,6},{5,7},{6,4},{7,5},{8,10},{9,11},{10,... | collective-permute-start | bytes 115208 | tf_op jit(solution)/shard_map/ppermute | solution.py:240
  47.0 7.1 %collective-permute-start.10 = (bf16[2,72,256]{2,1,0:T(8,128)(2,1)S(1)}, bf16[2,72,256]{2,1,0:T(8,128)(2,1)S(1)}, u32[]{:S(2)}, u32[]{:S(2)}) collective-permute-start(bf16[2,72,256]{2,1,0:T(8,128)(2,1)S(1)} %get-tuple-element.33), channel_id=1, source_target_pairs={{0,3},{1,2},{2,1},{3,0},{4,7},{5,6},{6,5},{7,4},{8,11},{9,10},{10,... | collective-permute-start | bytes 221192 | tf_op jit(solution)/shard_map/ppermute | solution.py:240
  47.1 7.1 %collective-permute-start.9 = (bf16[2,72,256]{2,1,0:T(8,128)(2,1)S(1)}, bf16[2,72,256]{2,1,0:T(8,128)(2,1)S(1)}, u32[]{:S(2)}, u32[]{:S(2)}) collective-permute-start(bf16[2,72,256]{2,1,0:T(8,128)(2,1)S(1)} %get-tuple-element.34), channel_id=1, source_target_pairs={{0,2},{1,3},{2,0},{3,1},{4,6},{5,7},{6,4},{7,5},{8,10},{9,11},{10,... | collective-permute-start | bytes 221192 | tf_op jit(solution)/shard_map/ppermute | solution.py:240
  48.5 5.7 %collective-permute-start.8 = (bf16[2,72,256]{2,1,0:T(8,128)(2,1)S(1)}, bf16[2,72,256]{2,1,0:T(8,128)(2,1)S(1)}, u32[]{:S(2)}, u32[]{:S(2)}) collective-permute-start(bf16[2,72,256]{2,1,0:T(8,128)(2,1)S(1)} %get-tuple-element.35), channel_id=1, source_target_pairs={{0,1},{1,0},{2,3},{3,2},{4,5},{5,4},{6,7},{7,6},{8,9},{9,8},{10,11... | collective-permute-start | bytes 221192 | tf_op jit(solution)/shard_map/ppermute | solution.py:240
  49.0 5.2 %collective-permute-start.11 = (f32[40,240]{1,0:T(8,128)S(1)}, f32[40,240]{1,0:T(8,128)S(1)}, u32[]{:S(2)}, u32[]{:S(2)}) collective-permute-start(f32[40,240]{1,0:T(8,128)S(1)} %add.88), channel_id=1, source_target_pairs={{0,16},{4,20},{8,24},{12,28},{16,0},{20,4},{24,8},{28,12},{1,17},{... | collective-permute-start | bytes 115208 | tf_op jit(solution)/shard_map/ppermute | solution.py:240
  54.9 1.6 %collective-permute-start.12 = (f32[2,80,256]{2,1,0:T(8,128)S(1)}, f32[2,80,256]{2,1,0:T(8,128)S(1)}, u32[]{:S(2)}, u32[]{:S(2)}) collective-permute-start(f32[2,80,256]{2,1,0:T(8,128)S(1)} %slice.48), channel_id=1, source_target_pairs={{0,1},{1,0},{2,3},{3,2},{4,5},{5,4},{6,7},{7,6},{8,9},{9,8},{10,11... | collective-permute-start | bytes 491528 | tf_op jit(solution)/shard_map/ppermute | solution.py:240
  55.1 4.1 %collective-permute-start.14 = (f32[40,240]{1,0:T(8,128)S(1)}, f32[40,240]{1,0:T(8,128)S(1)}, u32[]{:S(2)}, u32[]{:S(2)}) collective-permute-start(f32[40,240]{1,0:T(8,128)S(1)} %add.89), channel_id=1, source_target_pairs={{0,8},{4,12},{8,0},{12,4},{16,24},{20,28},{24,16},{28,20},{1,9},{5... | collective-permute-start | bytes 115208 | tf_op jit(solution)/shard_map/ppermute | solution.py:240
  56.6 4.6 %collective-permute-start.13 = (bf16[2,80,256]{2,1,0:T(8,128)(2,1)S(1)}, bf16[2,80,256]{2,1,0:T(8,128)(2,1)S(1)}, u32[]{:S(2)}, u32[]{:S(2)}) collective-permute-start(bf16[2,80,256]{2,1,0:T(8,128)(2,1)S(1)} %add_convert_fusion), channel_id=1, source_target_pairs={{0,2},{1,3},{2,0},{3,1},{4,6},{5,7},{6,4},{7,5},{8,10},{9,11},{10,... | collective-permute-start | bytes 245768 | tf_op jit(solution)/shard_map/ppermute | solution.py:240
  61.6 1.2 %collective-permute-start.16 = (f32[40,120]{1,0:T(8,128)S(1)}, f32[40,120]{1,0:T(8,128)S(1)}, u32[]{:S(2)}, u32[]{:S(2)}) collective-permute-start(f32[40,120]{1,0:T(8,128)S(1)} %gram_two.1), channel_id=1, source_target_pairs={{0,1},{1,0},{2,3},{3,2},{4,5},{5,4},{6,7},{7,6},{8,9},{9,8},{10,11... | collective-permute-start | bytes 57608 | tf_op jit(solution)/shard_map/ppermute | solution.py:240
  61.7 8.1 %collective-permute-start.17 = (f32[2,80,256]{2,1,0:T(8,128)S(1)}, f32[2,80,256]{2,1,0:T(8,128)S(1)}, u32[]{:S(2)}, u32[]{:S(2)}) collective-permute-start(f32[2,80,256]{2,1,0:T(8,128)S(1)} %pad_maximum_fusion.4.p_ref), channel_id=1, source_target_pairs={{0,1},{1,0},{2,3},{3,2},{4,5},{5,4},{6,7},{7,6},{8,9},{9,8},{10,11... | collective-permute-start | bytes 491528 | tf_op jit(solution)/shard_map/ppermute | solution.py:240
  63.5 12.0 %all-to-all-start.2 = ((f32[8,40,120]{2,1,0:T(8,128)}), f32[8,40,120]{2,1,0:T(8,128)S(1)}, u32[]{:S(2)}, u32[]{:S(2)}) async-start(f32[8,40,120]{2,1,0:T(8,128)} %broadcast_in_dim.11), calls=%async_computation.2 | async-start | bytes 327680 | tf_op jit(solution)/shard_map/all_to_all | solution.py:246
  67.7 4.9 %collective-permute-start.15 = (f32[40,240]{1,0:T(8,128)S(1)}, f32[40,240]{1,0:T(8,128)S(1)}, u32[]{:S(2)}, u32[]{:S(2)}) collective-permute-start(f32[40,240]{1,0:T(8,128)S(1)} %add.94), channel_id=1, source_target_pairs={{0,4},{4,0},{8,12},{12,8},{16,20},{20,16},{24,28},{28,24},{1,5},{5... | collective-permute-start | bytes 115208 | tf_op jit(solution)/shard_map/ppermute | solution.py:240
where the time goes:
time: 79.6 us; the launch traced here: 79.2 us
  starting transfers between devices  29.3 us (37%)
  waiting for transfers between devices  28.3 us (36%)
  Pallas kernels  15.9 us (20%)
  local copies, waits for them, and re-layouts  4.29 us (5%)
  between operations  1.08 us (1%)
    ppermute x18, waiting for transfers between devices, swap(): return lax.ppermute(array, axis, [(n, n ^ bit) for n in range(size)])  15.6 us
    ppermute x18, starting transfers between devices, swap(): return lax.ppermute(array, axis, [(n, n ^ bit) for n in range(size)])  14.1 us
    all_to_all x2, waiting for transfers between devices, body(): gathered = lax.all_to_all(copies, 'row', 0, 0)  11.6 us
    all_to_all x2, starting transfers between devices, body(): gathered = lax.all_to_all(copies, 'row', 0, 0)  11 us
    pallas_call x2, Pallas kernels, near(): pl.pallas_call(functools.partial(near_kernel, rows), in_specs=[pl.BlockSp...  8.25 us
    pallas_call x6, Pallas kernels, whole_call(): pl.pallas_call(kernel, in_specs=[vmem] * len(args), out_specs=vmem if sin...  7.64 us
    all_to_all x1, starting transfers between devices, spread(): return lax.all_to_all(copies, axis, 0, 0)  4.19 us
  transfers between devices with their start and end apart: 21, of which 11 were waited for; matrix products, arithmetic and copies ran while one was open for 1% of the time, Pallas kernels for 13%

commit v1 on v0

--- a/solution.py
+++ b/solution.py
@@ -50,7 +50,7 @@
             fetch(k, part).start()
     for k in range(slots):
         v = v_ref[(lax.axis_index("row") + k - slots // 2 + rows) % rows]
-        v = jnp.where(flags[:, k : k + 1] == 1, v.astype(F32), 0.0).astype(BF16)
+        v = jnp.where(flags[:, k : k + 1] > 0.5, v.astype(F32), 0.0).astype(BF16)
         for part in range(2):
             fetch(k, part).wait()
         for part, total in enumerate((first, second)):
@@ -275,7 +275,19 @@
 
     b_first = cut(incident, 0)
     copies = spread_start(sent(b_first), "row")
+    copies, incident, diagonal, harmonics, flags = lax.optimization_barrier(
+        (copies, incident, diagonal, harmonics, flags)
+    )
     gathered = lax.all_to_all(copies, "row", 0, 0)
+    used_slots = jnp.where(flags == 1, 1.0, 0.0)
+    b_all = jnp.stack([b_first] + [cut(incident, s) for s in range(1, cols)])
+    h_first = cut(harmonics, 0)
+    d_own = jnp.stack(
+        [lax.dynamic_slice_in_dim(diagonal, place(s), width, 0) for s in range(0, cols, 2)]
+    )
+    gathered, used_slots, b_all, h_first, d_own = lax.optimization_barrier(
+        (gathered, used_slots, b_all, h_first, d_own)
+    )
     rights = right_factors.reshape(blocks, 2 * rank, elements)
     lefts = left_factors.reshape(blocks * 2 * rank, elements)
 
@@ -286,7 +298,7 @@
             )
 
         pieces = [piece(0)] + [swap(piece(s), "col", s) for s in range(1, cols)]
-        total = near(flags, gathered, near_blocks, 2 * half)
+        total = near(used_slots, gathered, near_blocks, 2 * half)
         if one is not None:
             total, one = lax.optimization_barrier((total, one + swap(one, "row", row_bits[-1])))
         total = whole_call(
@@ -307,8 +319,7 @@
     for bit in reversed(bits[1:]):
         n = total.shape[0] // 2
         total = total[:n] + swap(total[n:], "col", bit)
-    d_first = lax.dynamic_slice_in_dim(diagonal, place(0), width, 0)
-    p_first = total[0] + (d_first - SHIFT)[None, :] * b_first
+    p_first = total[0] + (d_own[0] - SHIFT)[None, :] * b_first
 
     copies = spread_start(sent(p_first), "row")
     copies, p_early = lax.optimization_barrier((copies, p_first))
@@ -320,11 +331,10 @@
         "gram_one",
         b_first,
         p_early,
-        cut(harmonics, 0),
+        h_first,
     )
     for bit in bits:
         one = one + swap(one, "col", bit)
-    b_all = jnp.stack([b_first] + [cut(incident, s) for s in range(1, cols)])
     b_own = b_all[0::2]
     p_own = p_early[None]
     for bit in bits[1:]:
@@ -340,11 +350,7 @@
         other = swap(total, "col", bit).astype(F32)
         total = total.astype(F32) + jnp.stack([other[s ^ (bit // 2)] for s in range(cols // 2)])
         total = total if bit == bits[-1] else total.astype(BF16)
-    d_own = jnp.stack(
-        [lax.dynamic_slice_in_dim(diagonal, place(s), width, 0) for s in range(0, cols, 2)]
-    )
-    ap, one = lax.optimization_barrier((total + d_own[:, None, :] * p_own, one))
-    one = one + swap(one, "row", row_bits[0])
+    ap = total + d_own[:, None, :] * p_own
     two = whole_call(
         functools.partial(gram_two_kernel, SHIFT),
         jax.ShapeDtypeStruct((half, 3 * half), F32),
@@ -353,7 +359,9 @@
         p_own,
         ap,
     )
-    two = spread(two + swap(two, "col", 1), "row")
+    two, one = lax.optimization_barrier((two + swap(two, "col", 1), one))
+    one = one + swap(one, "row", row_bits[0])
+    two = spread(two, "row")
     inverse = whole_call(
         functools.partial(invert_kernel, fields),
         jax.ShapeDtypeStruct((half, 2 * half), F32),

time: 79.6 us -> 78.4 us (0.985)
  waiting for transfers between devices: 28.3 us -> 26.5 us
  starting transfers between devices: 29.3 us -> 28.1 us
  local copies, waits for them, and re-layouts: 4.29 us -> 5.31 us
    all_to_all x2, waiting for transfers between devices: 11.6 us -> 8.76 us  [body(): gathered = lax.all_to_all(copies, 'row', 0, 0)]
    ppermute x18, waiting for transfers between devices: 15.6 us -> 16.7 us  [swap(): return lax.ppermute(array, axis, [(n, n ^ bit) for n in range(size)])]
    dynamic_slice x0 -> x1, local copies, waits for them, and re-layouts: none -> 0.84 us  [body(): lax.dynamic_slice_in_dim(diagonal, place(s), width, 0)]
    dynamic_slice x1 -> x2, local copies, waits for them, and re-layouts: 1.25 us -> 2.08 us  [cut(): piece = lax.dynamic_slice_in_dim(array, place(s), width, 2)]
    ppermute x18, starting transfers between devices: 14.1 us -> 13.3 us  [swap(): return lax.ppermute(array, axis, [(n, n ^ bit) for n in range(size)])]
  transfers between devices with their start and end apart: 21 -> 21, of which waited for: 11 -> 13; matrix products, arithmetic and copies ran while one was open for 1% -> 5% of each run, Pallas kernels for 13% -> 14%
where the time goes in v1:
time: 78.4 us; the launch traced here: 77.8 us
  starting transfers between devices  28.1 us (36%)
  waiting for transfers between devices  26.5 us (34%)
  Pallas kernels  15.9 us (20%)
  local copies, waits for them, and re-layouts  5.31 us (7%)
  between operations  1.05 us (1%)
  other arithmetic  0.99 us (1%)
    ppermute x18, waiting for transfers between devices, swap(): return lax.ppermute(array, axis, [(n, n ^ bit) for n in range(size)])  16.7 us
    ppermute x18, starting transfers between devices, swap(): return lax.ppermute(array, axis, [(n, n ^ bit) for n in range(size)])  13.3 us
    all_to_all x2, starting transfers between devices, body(): gathered = lax.all_to_all(copies, 'row', 0, 0)  10.8 us
    all_to_all x2, waiting for transfers between devices, body(): gathered = lax.all_to_all(copies, 'row', 0, 0)  8.76 us
    pallas_call x2, Pallas kernels, near(): pl.pallas_call(functools.partial(near_kernel, rows), in_specs=[pl.BlockSp...  8.24 us
    pallas_call x6, Pallas kernels, whole_call(): pl.pallas_call(kernel, in_specs=[vmem] * len(args), out_specs=vmem if sin...  7.64 us
    all_to_all x1, starting transfers between devices, spread(): return lax.all_to_all(copies, axis, 0, 0)  3.95 us
    dynamic_slice x2, local copies, waits for them, and re-layouts, cut(): piece = lax.dynamic_slice_in_dim(array, place(s), width, 2)  2.08 us
  transfers between devices with their start and end apart: 21, of which 13 were waited for; matrix products, arithmetic and copies ran while one was open for 5% of the time, Pallas kernels for 14%

profile of v1, /device:TPU:0, one launch (start us, length us, event | category | flops | bytes accessed | tf_op | source)
XLA Modules:
  0.0 77.8 jit_solution(17372131951406441942)
XLA Ops:
  0.6 0.0 copy-start.2
  0.6 0.0 copy-start.3
  0.7 0.0 copy-start
  0.7 0.0 copy-start.1
  0.7 1.0 %constant_dynamic-slice_fusion.10 = f32[2,36,256]{2,0,1:T(2,128)S(1)} fusion(f32[2,36,1024]{2,0,1:T(2,128)} %param.8, s32[]{:T(128)S(6)} %select_n.35), kind=kLoop, calls=%fused_computation.26 | loop fusion | bytes 147460 | tf_op jit(solution)/shard_map/dynamic_slice | solution.py:268
  1.7 0.7 broadcast_in_dim.16
  2.5 7.3 %all-to-all-start = ((bf16[8,72,256]{2,1,0:T(8,128)(2,1)}), bf16[8,72,256]{2,1,0:T(8,128)(2,1)S(1)}, u32[]{:S(2)}, u32[]{:S(2)}) async-start(bf16[8,72,256]{2,1,0:T(8,128)(2,1)} %broadcast_in_dim.16), calls=%async_computation | async-start | bytes 589824 | tf_op jit(solution)/shard_map/all_to_all | solution.py:281
  9.7 1.1 %constant_dynamic-slice_fusion.9 = (f32[2,36,256]{2,0,1:T(2,128)S(1)}, f32[2,36,256]{2,0,1:T(2,128)S(1)}, f32[2,36,256]{2,0,1:T(2,128)S(1)}, f32[2,36,256]{2,0,1:T(2,128)S(1)}) fusion(f32[2,36,1024]{2,0,1:T(2,128)} %param.8, s32[]{:T(128)S(6)} %select_n.37, s32[]{:T(128)S(6)} %select_n.39, s32[]{:T(128)S(6)} %select_n.38, f32[2,36,1024]{2,0,1:T(2,128)} %param.15, ...), kind=kLoop, calls=%fused_computation.25 | loop fusion | bytes 589840 | tf_op jit(solution)/shard_map/dynamic_slice | solution.py:268
  11.0 0.8 %fusion.8 = (f32[256]{0:T(256)S(1)}, f32[256]{0:T(256)S(1)}) fusion(f32[1024]{0:T(1024)} %param.9, s32[]{:T(128)S(6)} %select_n.35, s32[]{:T(128)S(6)} %select_n.38), kind=kLoop, calls=%fused_computation.35 | loop fusion | bytes 4104 | tf_op jit(solution)/shard_map/dynamic_slice | solution.py:286
  11.9 0.7 compare_select_fusion.flags
  12.5 6.8 %all-to-all-done.v_ref = bf16[8,72,256]{2,1,0:T(8,128)(2,1)S(1)} async-done(((bf16[8,72,256]{2,1,0:T(8,128)(2,1)}), bf16[8,72,256]{2,1,0:T(8,128)(2,1)S(1)}, u32[]{:S(2)}, u32[]{:S(2)}) %all-to-all-start) | async-done | bytes 294944 | tf_op jit(solution)/shard_map/all_to_all | solution.py:281
  19.4 0.1 collective-permute-start.2
  19.4 1.6 %collective-permute-start.1 = (bf16[2,72,256]{2,1,0:T(8,128)(2,1)S(1)}, bf16[2,72,256]{2,1,0:T(8,128)(2,1)S(1)}, u32[]{:S(2)}, u32[]{:S(2)}) collective-permute-start(bf16[2,72,256]{2,1,0:T(8,128)(2,1)S(1)} %get-tuple-element.52), channel_id=1, source_target_pairs={{0,2},{1,3},{2,0},{3,1},{4,6},{5,7},{6,4},{7,5},{8,10},{9,11},{10,... | collective-permute-start | bytes 221192 | tf_op jit(solution)/shard_map/ppermute | solution.py:240
  21.0 0.3 collective-permute-start
  21.3 4.1 %near.2.near_ref = f32[80,1024]{1,0:T(8,128)S(1)} custom-call(f32[1,8]{1,0:T(1,128)S(1)} %compare_select_fusion.flags, bf16[8,72,256]{2,1,0:T(8,128)(2,1)S(1)} %all-to-all-done.v_ref, bf16[1,8,2,1024,256]{4,3,2,1,0:T(8,128)(2,1)} %blocks_ref.3), custom_call_target="tpu_custom_call" | custom-call | tf_op jit(solution)/shard_map/near/pallas_call | solution.py:71
  25.4 0.0 collective-permute-done.2
  25.4 0.1 collective-permute-done.1
  25.6 0.0 collective-permute-done
  25.6 0.0 copy-done.2
  25.6 0.0 copy-done.3
  25.6 0.0 copy-done
  25.7 0.6 far.2
  26.3 0.2 collective-permute-start.3
  26.5 1.3 %collective-permute-done.3 = f32[2,80,256]{2,1,0:T(8,128)S(1)} collective-permute-done((f32[2,80,256]{2,1,0:T(8,128)S(1)}, f32[2,80,256]{2,1,0:T(8,128)S(1)}, u32[]{:S(2)}, u32[]{:S(2)}) %collective-permute-start.3) | collective-permute-done | bytes 163872 | tf_op jit(solution)/shard_map/ppermute | solution.py:240
  27.8 1.5 %collective-permute-start.4 = (f32[1,80,256]{2,1,0:T(8,128)S(1)}, f32[1,80,256]{2,1,0:T(8,128)S(1)}, u32[]{:S(2)}, u32[]{:S(2)}) collective-permute-start(f32[1,80,256]{2,1,0:T(8,128)S(1)} %slice.59), channel_id=1, source_target_pairs={{0,2},{1,3},{2,0},{3,1},{4,6},{5,7},{6,4},{7,5},{8,10},{9,11},{10,... | collective-permute-start | bytes 245768 | tf_op jit(solution)/shard_map/ppermute | solution.py:240
  29.3 3.1 %collective-permute-done.4 = f32[1,80,256]{2,1,0:T(8,128)S(1)} collective-permute-done((f32[1,80,256]{2,1,0:T(8,128)S(1)}, f32[1,80,256]{2,1,0:T(8,128)S(1)}, u32[]{:S(2)}, u32[]{:S(2)}) %collective-permute-start.4) | collective-permute-done | bytes 81952 | tf_op jit(solution)/shard_map/ppermute | solution.py:240
  32.4 0.7 broadcast_in_dim.34
  33.2 3.6 %all-to-all-start.1 = ((bf16[8,72,256]{2,1,0:T(8,128)(2,1)}), bf16[8,72,256]{2,1,0:T(8,128)(2,1)S(1)}, u32[]{:S(2)}, u32[]{:S(2)}) async-start(bf16[8,72,256]{2,1,0:T(8,128)(2,1)} %broadcast_in_dim.34), calls=%async_computation.1 | async-start | bytes 589824 | tf_op jit(solution)/shard_map/all_to_all | solution.py:326
  36.8 1.4 %collective-permute-start.7 = (f32[1,80,256]{2,1,0:T(8,128)S(1)}, f32[1,80,256]{2,1,0:T(8,128)S(1)}, u32[]{:S(2)}, u32[]{:S(2)}) collective-permute-start(f32[1,80,256]{2,1,0:T(8,128)S(1)} %bitcast.43), channel_id=1, source_target_pairs={{0,2},{1,3},{2,0},{3,1},{4,6},{5,7},{6,4},{7,5},{8,10},{9,11},{10,... | collective-permute-start | bytes 245768 | tf_op jit(solution)/shard_map/ppermute | solution.py:240
  38.2 0.4 gram_one.1
  38.6 0.1 collective-permute-start.5
  38.7 1.2 %collective-permute-done.5 = f32[40,240]{1,0:T(8,128)S(1)} collective-permute-done((f32[40,240]{1,0:T(8,128)S(1)}, f32[40,240]{1,0:T(8,128)S(1)}, u32[]{:S(2)}, u32[]{:S(2)}) %collective-permute-start.5) | collective-permute-done | bytes 38432 | tf_op jit(solution)/shard_map/ppermute | solution.py:240
  39.9 0.6 collective-permute-start.6
  40.5 3.4 %collective-permute-done.6 = f32[40,240]{1,0:T(8,128)S(1)} collective-permute-done((f32[40,240]{1,0:T(8,128)S(1)}, f32[40,240]{1,0:T(8,128)S(1)}, u32[]{:S(2)}, u32[]{:S(2)}) %collective-permute-start.6) | collective-permute-done | bytes 38432 | tf_op jit(solution)/shard_map/ppermute | solution.py:240
  43.9 0.0 collective-permute-done.7
  43.9 1.9 %all-to-all-done.1.v_ref = bf16[8,72,256]{2,1,0:T(8,128)(2,1)S(1)} async-done(((bf16[8,72,256]{2,1,0:T(8,128)(2,1)}), bf16[8,72,256]{2,1,0:T(8,128)(2,1)S(1)}, u32[]{:S(2)}, u32[]{:S(2)}) %all-to-all-start.1) | async-done | bytes 294944 | tf_op jit(solution)/shard_map/all_to_all | solution.py:326
  45.9 0.1 collective-permute-start.10
  45.9 1.5 %collective-permute-start.9 = (bf16[2,72,256]{2,1,0:T(8,128)(2,1)S(1)}, bf16[2,72,256]{2,1,0:T(8,128)(2,1)S(1)}, u32[]{:S(2)}, u32[]{:S(2)}) collective-permute-start(bf16[2,72,256]{2,1,0:T(8,128)(2,1)S(1)} %get-tuple-element.48), channel_id=1, source_target_pairs={{0,2},{1,3},{2,0},{3,1},{4,6},{5,7},{6,4},{7,5},{8,10},{9,11},{10,... | collective-permute-start | bytes 221192 | tf_op jit(solution)/shard_map/ppermute | solution.py:240
  47.4 0.4 collective-permute-start.8
  47.8 1.0 %collective-permute-start.11 = (f32[40,240]{1,0:T(8,128)S(1)}, f32[40,240]{1,0:T(8,128)S(1)}, u32[]{:S(2)}, u32[]{:S(2)}) collective-permute-start(f32[40,240]{1,0:T(8,128)S(1)} %add.91), channel_id=1, source_target_pairs={{0,16},{4,20},{8,24},{12,28},{16,0},{20,4},{24,8},{28,12},{1,17},{... | collective-permute-start | bytes 115208 | tf_op jit(solution)/shard_map/ppermute | solution.py:240
  48.8 4.1 %near.3.near_ref = f32[80,1024]{1,0:T(8,128)S(1)} custom-call(f32[1,8]{1,0:T(1,128)S(1)} %compare_select_fusion.flags, bf16[8,72,256]{2,1,0:T(8,128)(2,1)S(1)} %all-to-all-done.1.v_ref, bf16[1,8,2,1024,256]{4,3,2,1,0:T(8,128)(2,1)} %blocks_ref.3), custom_call_target="tpu_custom_call" | custom-call | tf_op jit(solution)/shard_map/near/pallas_call | solution.py:71
  53.0 0.3 collective-permute-done.11
  53.3 0.0 collective-permute-done.10
  53.3 0.0 collective-permute-done.9
  53.3 0.0 collective-permute-done.8
  53.4 0.6 far.3
  54.0 0.1 collective-permute-start.12
  54.1 1.4 %collective-permute-done.12 = f32[2,80,256]{2,1,0:T(8,128)S(1)} collective-permute-done((f32[2,80,256]{2,1,0:T(8,128)S(1)}, f32[2,80,256]{2,1,0:T(8,128)S(1)}, u32[]{:S(2)}, u32[]{:S(2)}) %collective-permute-start.12) | collective-permute-done | bytes 163872 | tf_op jit(solution)/shard_map/ppermute | solution.py:240
  55.5 1.2 %collective-permute-start.13 = (bf16[2,80,256]{2,1,0:T(8,128)(2,1)S(1)}, bf16[2,80,256]{2,1,0:T(8,128)(2,1)S(1)}, u32[]{:S(2)}, u32[]{:S(2)}) collective-permute-start(bf16[2,80,256]{2,1,0:T(8,128)(2,1)S(1)} %add_convert_fusion), channel_id=1, source_target_pairs={{0,2},{1,3},{2,0},{3,1},{4,6},{5,7},{6,4},{7,5},{8,10},{9,11},{10,... | collective-permute-start | bytes 245768 | tf_op jit(solution)/shard_map/ppermute | solution.py:240
  56.7 0.9 %collective-permute-start.15 = (f32[40,240]{1,0:T(8,128)S(1)}, f32[40,240]{1,0:T(8,128)S(1)}, u32[]{:S(2)}, u32[]{:S(2)}) collective-permute-start(f32[40,240]{1,0:T(8,128)S(1)} %add.92), channel_id=1, source_target_pairs={{0,8},{4,12},{8,0},{12,4},{16,24},{20,28},{24,16},{28,20},{1,9},{5... | collective-permute-start | bytes 115208 | tf_op jit(solution)/shard_map/ppermute | solution.py:240
  57.6 2.5 %collective-permute-done.13 = bf16[2,80,256]{2,1,0:T(8,128)(2,1)S(1)} collective-permute-done((bf16[2,80,256]{2,1,0:T(8,128)(2,1)S(1)}, bf16[2,80,256]{2,1,0:T(8,128)(2,1)S(1)}, u32[]{:S(2)}, u32[]{:S(2)}) %collective-permute-start.13) | collective-permute-done | bytes 81952 | tf_op jit(solution)/shard_map/ppermute | solution.py:240
  60.1 0.4 gram_two.1
  60.5 0.1 collective-permute-start.14
  60.5 0.5 collective-permute-start.17
  61.0 0.0 collective-permute-done.15
  61.1 0.7 collective-permute-done.14
  61.7 0.7 broadcast_in_dim.36
  62.4 3.9 %all-to-all-start.2 = ((f32[8,40,120]{2,1,0:T(8,128)}), f32[8,40,120]{2,1,0:T(8,128)S(1)}, u32[]{:S(2)}, u32[]{:S(2)}) async-start(f32[8,40,120]{2,1,0:T(8,128)} %broadcast_in_dim.36), calls=%async_computation.2 | async-start | bytes 327680 | tf_op jit(solution)/shard_map/all_to_all | solution.py:246
  66.4 2.0 %collective-permute-start.16 = (f32[40,240]{1,0:T(8,128)S(1)}, f32[40,240]{1,0:T(8,128)S(1)}, u32[]{:S(2)}, u32[]{:S(2)}) collective-permute-start(f32[40,240]{1,0:T(8,128)S(1)} %add.97), channel_id=1, source_target_pairs={{0,4},{4,0},{8,12},{12,8},{16,20},{20,16},{24,28},{28,24},{1,5},{5... | collective-permute-start | bytes 115208 | tf_op jit(solution)/shard_map/ppermute | solution.py:240
  68.4 0.0 collective-permute-done.17
  68.4 2.8 %collective-permute-done.16 = f32[40,240]{1,0:T(8,128)S(1)} collective-permute-done((f32[40,240]{1,0:T(8,128)S(1)}, f32[40,240]{1,0:T(8,128)S(1)}, u32[]{:S(2)}, u32[]{:S(2)}) %collective-permute-start.16) | collective-permute-done | bytes 38432 | tf_op jit(solution)/shard_map/ppermute | solution.py:240
  71.2 1.9 %invert.1.inv_ref = f32[40,80]{1,0:T(8,128)S(1)} custom-call(f32[40,240]{1,0:T(8,128)S(1)} %add.98.g1_ref), custom_call_target="tpu_custom_call" | custom-call | tf_op jit(solution)/shard_map/invert/pallas_call | solution.py:227
  73.2 1.0 %all-to-all-done.2.g2_ref = f32[8,40,120]{2,1,0:T(8,128)S(1)} async-done(((f32[8,40,120]{2,1,0:T(8,128)}), f32[8,40,120]{2,1,0:T(8,128)S(1)}, u32[]{:S(2)}, u32[]{:S(2)}) %all-to-all-start.2) | async-done | bytes 153632 | tf_op jit(solution)/shard_map/all_to_all | solution.py:246
  74.2 3.7 %solve.1 = (f32[36,2,1024]{2,1,0:T(2,128)}, f32[36,2,36]{2,1,0:T(2,128)}) custom-call(f32[40,80]{1,0:T(8,128)S(1)} %invert.1.inv_ref, f32[40,240]{1,0:T(8,128)S(1)} %add.98.g1_ref, f32[8,40,120]{2,1,0:T(8,128)S(1)} %all-to-all-done.2.g2_ref, f32[4,80,256]{2,1,0:T(8,128)S(1)} %pad_maximum_fusion.b_ref, f32[4,80,256]{2,1,0:T(8,128)S(1)} %bitcast.42), custom_call_target="tpu_custom_call" | custom-call | tf_op jit(solution)/shard_map/solve/pallas_call | solution.py:227
  (41 shorter events, 0.5 us)
Async XLA Ops:
  0.6 25.0 %copy-start.2 = (s32[1,8]{1,0:T(1,128)S(1)}, s32[1,8]{1,0:T(1,128)}, u32[]{:S(2)}) copy-start(s32[1,8]{1,0:T(1,128)} %flags.1) | copy-start | bytes 100
  0.6 25.0 %copy-start.3 = (s32[1,2]{1,0:T(1,128)S(1)}, s32[1,2]{1,0:T(1,128)}, u32[]{:S(2)}) copy-start(s32[1,2]{1,0:T(1,128)} %ranks.3) | copy-start | bytes 28
  0.7 25.0 %copy-start = (bf16[1,2,2,64,1024]{4,3,2,1,0:T(8,128)(2,1)S(1)}, bf16[1,2,2,64,1024]{4,3,2,1,0:T(8,128)(2,1)}, u32[]{:S(2)}) copy-start(bf16[1,2,2,64,1024]{4,3,2,1,0:T(8,128)(2,1)} %param.12) | copy-start | bytes 1572868
  0.7 25.0 %copy-start.1 = (bf16[1,2,2,64,1024]{4,3,2,1,0:T(8,128)(2,1)S(1)}, bf16[1,2,2,64,1024]{4,3,2,1,0:T(8,128)(2,1)}, u32[]{:S(2)}) copy-start(bf16[1,2,2,64,1024]{4,3,2,1,0:T(8,128)(2,1)} %param.11) | copy-start | bytes 1572868
  2.5 16.9 %all-to-all-start = ((bf16[8,72,256]{2,1,0:T(8,128)(2,1)}), bf16[8,72,256]{2,1,0:T(8,128)(2,1)S(1)}, u32[]{:S(2)}, u32[]{:S(2)}) async-start(bf16[8,72,256]{2,1,0:T(8,128)(2,1)} %broadcast_in_dim.16), calls=%async_computation | async-start | bytes 589824 | tf_op jit(solution)/shard_map/all_to_all | solution.py:281
  19.4 6.1 %collective-permute-start.2 = (bf16[2,72,256]{2,1,0:T(8,128)(2,1)S(1)}, bf16[2,72,256]{2,1,0:T(8,128)(2,1)S(1)}, u32[]{:S(2)}, u32[]{:S(2)}) collective-permute-start(bf16[2,72,256]{2,1,0:T(8,128)(2,1)S(1)} %get-tuple-element.51), channel_id=1, source_target_pairs={{0,3},{1,2},{2,1},{3,0},{4,7},{5,6},{6,5},{7,4},{8,11},{9,10},{10,... | collective-permute-start | bytes 221192 | tf_op jit(solution)/shard_map/ppermute | solution.py:240
  19.4 6.1 %collective-permute-start.1 = (bf16[2,72,256]{2,1,0:T(8,128)(2,1)S(1)}, bf16[2,72,256]{2,1,0:T(8,128)(2,1)S(1)}, u32[]{:S(2)}, u32[]{:S(2)}) collective-permute-start(bf16[2,72,256]{2,1,0:T(8,128)(2,1)S(1)} %get-tuple-element.52), channel_id=1, source_target_pairs={{0,2},{1,3},{2,0},{3,1},{4,6},{5,7},{6,4},{7,5},{8,10},{9,11},{10,... | collective-permute-start | bytes 221192 | tf_op jit(solution)/shard_map/ppermute | solution.py:240
  21.0 4.6 %collective-permute-start = (bf16[2,72,256]{2,1,0:T(8,128)(2,1)S(1)}, bf16[2,72,256]{2,1,0:T(8,128)(2,1)S(1)}, u32[]{:S(2)}, u32[]{:S(2)}) collective-permute-start(bf16[2,72,256]{2,1,0:T(8,128)(2,1)S(1)} %get-tuple-element.53), channel_id=1, source_target_pairs={{0,1},{1,0},{2,3},{3,2},{4,5},{5,4},{6,7},{7,6},{8,9},{9,8},{10,11... | collective-permute-start | bytes 221192 | tf_op jit(solution)/shard_map/ppermute | solution.py:240
  26.3 1.5 %collective-permute-start.3 = (f32[2,80,256]{2,1,0:T(8,128)S(1)}, f32[2,80,256]{2,1,0:T(8,128)S(1)}, u32[]{:S(2)}, u32[]{:S(2)}) collective-permute-start(f32[2,80,256]{2,1,0:T(8,128)S(1)} %slice.46), channel_id=1, source_target_pairs={{0,1},{1,0},{2,3},{3,2},{4,5},{5,4},{6,7},{7,6},{8,9},{9,8},{10,11... | collective-permute-start | bytes 491528 | tf_op jit(solution)/shard_map/ppermute | solution.py:240
  27.8 4.6 %collective-permute-start.4 = (f32[1,80,256]{2,1,0:T(8,128)S(1)}, f32[1,80,256]{2,1,0:T(8,128)S(1)}, u32[]{:S(2)}, u32[]{:S(2)}) collective-permute-start(f32[1,80,256]{2,1,0:T(8,128)S(1)} %slice.59), channel_id=1, source_target_pairs={{0,2},{1,3},{2,0},{3,1},{4,6},{5,7},{6,4},{7,5},{8,10},{9,11},{10,... | collective-permute-start | bytes 245768 | tf_op jit(solution)/shard_map/ppermute | solution.py:240
  33.2 12.7 %all-to-all-start.1 = ((bf16[8,72,256]{2,1,0:T(8,128)(2,1)}), bf16[8,72,256]{2,1,0:T(8,128)(2,1)S(1)}, u32[]{:S(2)}, u32[]{:S(2)}) async-start(bf16[8,72,256]{2,1,0:T(8,128)(2,1)} %broadcast_in_dim.34), calls=%async_computation.1 | async-start | bytes 589824 | tf_op jit(solution)/shard_map/all_to_all | solution.py:326
  36.8 7.1 %collective-permute-start.7 = (f32[1,80,256]{2,1,0:T(8,128)S(1)}, f32[1,80,256]{2,1,0:T(8,128)S(1)}, u32[]{:S(2)}, u32[]{:S(2)}) collective-permute-start(f32[1,80,256]{2,1,0:T(8,128)S(1)} %bitcast.43), channel_id=1, source_target_pairs={{0,2},{1,3},{2,0},{3,1},{4,6},{5,7},{6,4},{7,5},{8,10},{9,11},{10,... | collective-permute-start | bytes 245768 | tf_op jit(solution)/shard_map/ppermute | solution.py:240
  38.6 1.3 %collective-permute-start.5 = (f32[40,240]{1,0:T(8,128)S(1)}, f32[40,240]{1,0:T(8,128)S(1)}, u32[]{:S(2)}, u32[]{:S(2)}) collective-permute-start(f32[40,240]{1,0:T(8,128)S(1)} %gram_one.1), channel_id=1, source_target_pairs={{0,1},{1,0},{2,3},{3,2},{4,5},{5,4},{6,7},{7,6},{8,9},{9,8},{10,11... | collective-permute-start | bytes 115208 | tf_op jit(solution)/shard_map/ppermute | solution.py:240
  39.9 4.0 %collective-permute-start.6 = (f32[40,240]{1,0:T(8,128)S(1)}, f32[40,240]{1,0:T(8,128)S(1)}, u32[]{:S(2)}, u32[]{:S(2)}) collective-permute-start(f32[40,240]{1,0:T(8,128)S(1)} %add.90), channel_id=1, source_target_pairs={{0,2},{1,3},{2,0},{3,1},{4,6},{5,7},{6,4},{7,5},{8,10},{9,11},{10,... | collective-permute-start | bytes 115208 | tf_op jit(solution)/shard_map/ppermute | solution.py:240
  45.9 7.4 %collective-permute-start.10 = (bf16[2,72,256]{2,1,0:T(8,128)(2,1)S(1)}, bf16[2,72,256]{2,1,0:T(8,128)(2,1)S(1)}, u32[]{:S(2)}, u32[]{:S(2)}) collective-permute-start(bf16[2,72,256]{2,1,0:T(8,128)(2,1)S(1)} %get-tuple-element.47), channel_id=1, source_target_pairs={{0,3},{1,2},{2,1},{3,0},{4,7},{5,6},{6,5},{7,4},{8,11},{9,10},{10,... | collective-permute-start | bytes 221192 | tf_op jit(solution)/shard_map/ppermute | solution.py:240
  45.9 7.3 %collective-permute-start.9 = (bf16[2,72,256]{2,1,0:T(8,128)(2,1)S(1)}, bf16[2,72,256]{2,1,0:T(8,128)(2,1)S(1)}, u32[]{:S(2)}, u32[]{:S(2)}) collective-permute-start(bf16[2,72,256]{2,1,0:T(8,128)(2,1)S(1)} %get-tuple-element.48), channel_id=1, source_target_pairs={{0,2},{1,3},{2,0},{3,1},{4,6},{5,7},{6,4},{7,5},{8,10},{9,11},{10,... | collective-permute-start | bytes 221192 | tf_op jit(solution)/shard_map/ppermute | solution.py:240
  47.4 5.9 %collective-permute-start.8 = (bf16[2,72,256]{2,1,0:T(8,128)(2,1)S(1)}, bf16[2,72,256]{2,1,0:T(8,128)(2,1)S(1)}, u32[]{:S(2)}, u32[]{:S(2)}) collective-permute-start(bf16[2,72,256]{2,1,0:T(8,128)(2,1)S(1)} %get-tuple-element.49), channel_id=1, source_target_pairs={{0,1},{1,0},{2,3},{3,2},{4,5},{5,4},{6,7},{7,6},{8,9},{9,8},{10,11... | collective-permute-start | bytes 221192 | tf_op jit(solution)/shard_map/ppermute | solution.py:240
  47.8 5.5 %collective-permute-start.11 = (f32[40,240]{1,0:T(8,128)S(1)}, f32[40,240]{1,0:T(8,128)S(1)}, u32[]{:S(2)}, u32[]{:S(2)}) collective-permute-start(f32[40,240]{1,0:T(8,128)S(1)} %add.91), channel_id=1, source_target_pairs={{0,16},{4,20},{8,24},{12,28},{16,0},{20,4},{24,8},{28,12},{1,17},{... | collective-permute-start | bytes 115208 | tf_op jit(solution)/shard_map/ppermute | solution.py:240
  54.0 1.5 %collective-permute-start.12 = (f32[2,80,256]{2,1,0:T(8,128)S(1)}, f32[2,80,256]{2,1,0:T(8,128)S(1)}, u32[]{:S(2)}, u32[]{:S(2)}) collective-permute-start(f32[2,80,256]{2,1,0:T(8,128)S(1)} %slice.53), channel_id=1, source_target_pairs={{0,1},{1,0},{2,3},{3,2},{4,5},{5,4},{6,7},{7,6},{8,9},{9,8},{10,11... | collective-permute-start | bytes 491528 | tf_op jit(solution)/shard_map/ppermute | solution.py:240
  55.5 4.6 %collective-permute-start.13 = (bf16[2,80,256]{2,1,0:T(8,128)(2,1)S(1)}, bf16[2,80,256]{2,1,0:T(8,128)(2,1)S(1)}, u32[]{:S(2)}, u32[]{:S(2)}) collective-permute-start(bf16[2,80,256]{2,1,0:T(8,128)(2,1)S(1)} %add_convert_fusion), channel_id=1, source_target_pairs={{0,2},{1,3},{2,0},{3,1},{4,6},{5,7},{6,4},{7,5},{8,10},{9,11},{10,... | collective-permute-start | bytes 245768 | tf_op jit(solution)/shard_map/ppermute | solution.py:240
  56.7 4.4 %collective-permute-start.15 = (f32[40,240]{1,0:T(8,128)S(1)}, f32[40,240]{1,0:T(8,128)S(1)}, u32[]{:S(2)}, u32[]{:S(2)}) collective-permute-start(f32[40,240]{1,0:T(8,128)S(1)} %add.92), channel_id=1, source_target_pairs={{0,8},{4,12},{8,0},{12,4},{16,24},{20,28},{24,16},{28,20},{1,9},{5... | collective-permute-start | bytes 115208 | tf_op jit(solution)/shard_map/ppermute | solution.py:240
  60.5 1.2 %collective-permute-start.14 = (f32[40,120]{1,0:T(8,128)S(1)}, f32[40,120]{1,0:T(8,128)S(1)}, u32[]{:S(2)}, u32[]{:S(2)}) collective-permute-start(f32[40,120]{1,0:T(8,128)S(1)} %gram_two.1), channel_id=1, source_target_pairs={{0,1},{1,0},{2,3},{3,2},{4,5},{5,4},{6,7},{7,6},{8,9},{9,8},{10,11... | collective-permute-start | bytes 57608 | tf_op jit(solution)/shard_map/ppermute | solution.py:240
  60.5 7.8 %collective-permute-start.17 = (f32[2,80,256]{2,1,0:T(8,128)S(1)}, f32[2,80,256]{2,1,0:T(8,128)S(1)}, u32[]{:S(2)}, u32[]{:S(2)}) collective-permute-start(f32[2,80,256]{2,1,0:T(8,128)S(1)} %pad_maximum_fusion.4.p_ref), channel_id=1, source_target_pairs={{0,1},{1,0},{2,3},{3,2},{4,5},{5,4},{6,7},{7,6},{8,9},{9,8},{10,11... | collective-permute-start | bytes 491528 | tf_op jit(solution)/shard_map/ppermute | solution.py:240
  62.4 11.7 %all-to-all-start.2 = ((f32[8,40,120]{2,1,0:T(8,128)}), f32[8,40,120]{2,1,0:T(8,128)S(1)}, u32[]{:S(2)}, u32[]{:S(2)}) async-start(f32[8,40,120]{2,1,0:T(8,128)} %broadcast_in_dim.36), calls=%async_computation.2 | async-start | bytes 327680 | tf_op jit(solution)/shard_map/all_to_all | solution.py:246
  66.4 4.9 %collective-permute-start.16 = (f32[40,240]{1,0:T(8,128)S(1)}, f32[40,240]{1,0:T(8,128)S(1)}, u32[]{:S(2)}, u32[]{:S(2)}) collective-permute-start(f32[40,240]{1,0:T(8,128)S(1)} %add.97), channel_id=1, source_target_pairs={{0,4},{4,0},{8,12},{12,8},{16,20},{20,16},{24,28},{28,24},{1,5},{5... | collective-permute-start | bytes 115208 | tf_op jit(solution)/shard_map/ppermute | solution.py:240

commit v2 on v1

--- a/solution.py
+++ b/solution.py
@@ -299,8 +299,6 @@
 
         pieces = [piece(0)] + [swap(piece(s), "col", s) for s in range(1, cols)]
         total = near(used_slots, gathered, near_blocks, 2 * half)
-        if one is not None:
-            total, one = lax.optimization_barrier((total, one + swap(one, "row", row_bits[-1])))
         total = whole_call(
             functools.partial(far_kernel, rows),
             jax.ShapeDtypeStruct((cols, 2 * half, width), F32),
@@ -312,7 +310,9 @@
             lefts,
             total,
         )
-        return total if one is None else (total, one)
+        if one is None:
+            return total
+        return lax.optimization_barrier((total, one + swap(one, "row", row_bits[-1])))
 
     total = operator(gathered)
     total = total[0::2] + swap(total[1::2], "col", 1)

time: 78.4 us -> 78.4 us (level)
  no operation moved by 1% of the time
where the time goes in v2:
time: 78.4 us; the launch traced here: 77.8 us
  starting transfers between devices  28.1 us (36%)
  waiting for transfers between devices  26.5 us (34%)
  Pallas kernels  15.9 us (20%)
  local copies, waits for them, and re-layouts  5.31 us (7%)
  between operations  1.05 us (1%)
  other arithmetic  0.99 us (1%)
    ppermute x18, waiting for transfers between devices, swap(): return lax.ppermute(array, axis, [(n, n ^ bit) for n in range(size)])  16.7 us
    ppermute x18, starting transfers between devices, swap(): return lax.ppermute(array, axis, [(n, n ^ bit) for n in range(size)])  13.3 us
    all_to_all x2, starting transfers between devices, body(): gathered = lax.all_to_all(copies, 'row', 0, 0)  10.8 us
    all_to_all x2, waiting for transfers between devices, body(): gathered = lax.all_to_all(copies, 'row', 0, 0)  8.76 us
    pallas_call x2, Pallas kernels, near(): pl.pallas_call(functools.partial(near_kernel, rows), in_specs=[pl.BlockSp...  8.24 us
    pallas_call x6, Pallas kernels, whole_call(): pl.pallas_call(kernel, in_specs=[vmem] * len(args), out_specs=vmem if sin...  7.64 us
    all_to_all x1, starting transfers between devices, spread(): return lax.all_to_all(copies, axis, 0, 0)  3.95 us
    dynamic_slice x2, local copies, waits for them, and re-layouts, cut(): piece = lax.dynamic_slice_in_dim(array, place(s), width, 2)  2.08 us
  transfers between devices with their start and end apart: 21, of which 13 were waited for; matrix products, arithmetic and copies ran while one was open for 5% of the time, Pallas kernels for 14%

profile of v2, /device:TPU:0, one launch (start us, length us, event | category | flops | bytes accessed | tf_op | source)
XLA Modules:
  0.0 77.8 jit_solution(17372131951406441942)
XLA Ops:
  0.6 0.0 copy-start.2
  0.6 0.0 copy-start.3
  0.7 0.0 copy-start
  0.7 0.0 copy-start.1
  0.7 1.0 %constant_dynamic-slice_fusion.10 = f32[2,36,256]{2,0,1:T(2,128)S(1)} fusion(f32[2,36,1024]{2,0,1:T(2,128)} %param.8, s32[]{:T(128)S(6)} %select_n.35), kind=kLoop, calls=%fused_computation.26 | loop fusion | bytes 147460 | tf_op jit(solution)/shard_map/dynamic_slice | solution.py:268
  1.7 0.7 broadcast_in_dim.16
  2.5 7.3 %all-to-all-start = ((bf16[8,72,256]{2,1,0:T(8,128)(2,1)}), bf16[8,72,256]{2,1,0:T(8,128)(2,1)S(1)}, u32[]{:S(2)}, u32[]{:S(2)}) async-start(bf16[8,72,256]{2,1,0:T(8,128)(2,1)} %broadcast_in_dim.16), calls=%async_computation | async-start | bytes 589824 | tf_op jit(solution)/shard_map/all_to_all | solution.py:281
  9.7 1.1 %constant_dynamic-slice_fusion.9 = (f32[2,36,256]{2,0,1:T(2,128)S(1)}, f32[2,36,256]{2,0,1:T(2,128)S(1)}, f32[2,36,256]{2,0,1:T(2,128)S(1)}, f32[2,36,256]{2,0,1:T(2,128)S(1)}) fusion(f32[2,36,1024]{2,0,1:T(2,128)} %param.8, s32[]{:T(128)S(6)} %select_n.37, s32[]{:T(128)S(6)} %select_n.39, s32[]{:T(128)S(6)} %select_n.38, f32[2,36,1024]{2,0,1:T(2,128)} %param.15, ...), kind=kLoop, calls=%fused_computation.25 | loop fusion | bytes 589840 | tf_op jit(solution)/shard_map/dynamic_slice | solution.py:268
  11.0 0.8 %fusion.8 = (f32[256]{0:T(256)S(1)}, f32[256]{0:T(256)S(1)}) fusion(f32[1024]{0:T(1024)} %param.9, s32[]{:T(128)S(6)} %select_n.35, s32[]{:T(128)S(6)} %select_n.38), kind=kLoop, calls=%fused_computation.35 | loop fusion | bytes 4104 | tf_op jit(solution)/shard_map/dynamic_slice | solution.py:286
  11.9 0.7 compare_select_fusion.flags
  12.5 6.8 %all-to-all-done.v_ref = bf16[8,72,256]{2,1,0:T(8,128)(2,1)S(1)} async-done(((bf16[8,72,256]{2,1,0:T(8,128)(2,1)}), bf16[8,72,256]{2,1,0:T(8,128)(2,1)S(1)}, u32[]{:S(2)}, u32[]{:S(2)}) %all-to-all-start) | async-done | bytes 294944 | tf_op jit(solution)/shard_map/all_to_all | solution.py:281
  19.4 0.1 collective-permute-start.2
  19.4 1.6 %collective-permute-start.1 = (bf16[2,72,256]{2,1,0:T(8,128)(2,1)S(1)}, bf16[2,72,256]{2,1,0:T(8,128)(2,1)S(1)}, u32[]{:S(2)}, u32[]{:S(2)}) collective-permute-start(bf16[2,72,256]{2,1,0:T(8,128)(2,1)S(1)} %get-tuple-element.52), channel_id=1, source_target_pairs={{0,2},{1,3},{2,0},{3,1},{4,6},{5,7},{6,4},{7,5},{8,10},{9,11},{10,... | collective-permute-start | bytes 221192 | tf_op jit(solution)/shard_map/ppermute | solution.py:240
  21.0 0.3 collective-permute-start
  21.3 4.1 %near.2.near_ref = f32[80,1024]{1,0:T(8,128)S(1)} custom-call(f32[1,8]{1,0:T(1,128)S(1)} %compare_select_fusion.flags, bf16[8,72,256]{2,1,0:T(8,128)(2,1)S(1)} %all-to-all-done.v_ref, bf16[1,8,2,1024,256]{4,3,2,1,0:T(8,128)(2,1)} %blocks_ref.3), custom_call_target="tpu_custom_call" | custom-call | tf_op jit(solution)/shard_map/near/pallas_call | solution.py:71
  25.4 0.0 collective-permute-done.2
  25.4 0.1 collective-permute-done.1
  25.6 0.0 collective-permute-done
  25.6 0.0 copy-done.2
  25.6 0.0 copy-done.3
  25.6 0.0 copy-done
  25.7 0.6 far.2
  26.3 0.2 collective-permute-start.3
  26.5 1.3 %collective-permute-done.3 = f32[2,80,256]{2,1,0:T(8,128)S(1)} collective-permute-done((f32[2,80,256]{2,1,0:T(8,128)S(1)}, f32[2,80,256]{2,1,0:T(8,128)S(1)}, u32[]{:S(2)}, u32[]{:S(2)}) %collective-permute-start.3) | collective-permute-done | bytes 163872 | tf_op jit(solution)/shard_map/ppermute | solution.py:240
  27.8 1.5 %collective-permute-start.4 = (f32[1,80,256]{2,1,0:T(8,128)S(1)}, f32[1,80,256]{2,1,0:T(8,128)S(1)}, u32[]{:S(2)}, u32[]{:S(2)}) collective-permute-start(f32[1,80,256]{2,1,0:T(8,128)S(1)} %slice.59), channel_id=1, source_target_pairs={{0,2},{1,3},{2,0},{3,1},{4,6},{5,7},{6,4},{7,5},{8,10},{9,11},{10,... | collective-permute-start | bytes 245768 | tf_op jit(solution)/shard_map/ppermute | solution.py:240
  29.3 3.1 %collective-permute-done.4 = f32[1,80,256]{2,1,0:T(8,128)S(1)} collective-permute-done((f32[1,80,256]{2,1,0:T(8,128)S(1)}, f32[1,80,256]{2,1,0:T(8,128)S(1)}, u32[]{:S(2)}, u32[]{:S(2)}) %collective-permute-start.4) | collective-permute-done | bytes 81952 | tf_op jit(solution)/shard_map/ppermute | solution.py:240
  32.4 0.7 broadcast_in_dim.34
  33.2 3.6 %all-to-all-start.1 = ((bf16[8,72,256]{2,1,0:T(8,128)(2,1)}), bf16[8,72,256]{2,1,0:T(8,128)(2,1)S(1)}, u32[]{:S(2)}, u32[]{:S(2)}) async-start(bf16[8,72,256]{2,1,0:T(8,128)(2,1)} %broadcast_in_dim.34), calls=%async_computation.1 | async-start | bytes 589824 | tf_op jit(solution)/shard_map/all_to_all | solution.py:326
  36.8 1.4 %collective-permute-start.7 = (f32[1,80,256]{2,1,0:T(8,128)S(1)}, f32[1,80,256]{2,1,0:T(8,128)S(1)}, u32[]{:S(2)}, u32[]{:S(2)}) collective-permute-start(f32[1,80,256]{2,1,0:T(8,128)S(1)} %bitcast.43), channel_id=1, source_target_pairs={{0,2},{1,3},{2,0},{3,1},{4,6},{5,7},{6,4},{7,5},{8,10},{9,11},{10,... | collective-permute-start | bytes 245768 | tf_op jit(solution)/shard_map/ppermute | solution.py:240
  38.2 0.4 gram_one.1
  38.6 0.1 collective-permute-start.5
  38.7 1.2 %collective-permute-done.5 = f32[40,240]{1,0:T(8,128)S(1)} collective-permute-done((f32[40,240]{1,0:T(8,128)S(1)}, f32[40,240]{1,0:T(8,128)S(1)}, u32[]{:S(2)}, u32[]{:S(2)}) %collective-permute-start.5) | collective-permute-done | bytes 38432 | tf_op jit(solution)/shard_map/ppermute | solution.py:240
  39.9 0.6 collective-permute-start.6
  40.5 3.4 %collective-permute-done.6 = f32[40,240]{1,0:T(8,128)S(1)} collective-permute-done((f32[40,240]{1,0:T(8,128)S(1)}, f32[40,240]{1,0:T(8,128)S(1)}, u32[]{:S(2)}, u32[]{:S(2)}) %collective-permute-start.6) | collective-permute-done | bytes 38432 | tf_op jit(solution)/shard_map/ppermute | solution.py:240
  43.9 0.0 collective-permute-done.7
  43.9 1.9 %all-to-all-done.1.v_ref = bf16[8,72,256]{2,1,0:T(8,128)(2,1)S(1)} async-done(((bf16[8,72,256]{2,1,0:T(8,128)(2,1)}), bf16[8,72,256]{2,1,0:T(8,128)(2,1)S(1)}, u32[]{:S(2)}, u32[]{:S(2)}) %all-to-all-start.1) | async-done | bytes 294944 | tf_op jit(solution)/shard_map/all_to_all | solution.py:326
  45.9 0.1 collective-permute-start.10
  45.9 1.5 %collective-permute-start.9 = (bf16[2,72,256]{2,1,0:T(8,128)(2,1)S(1)}, bf16[2,72,256]{2,1,0:T(8,128)(2,1)S(1)}, u32[]{:S(2)}, u32[]{:S(2)}) collective-permute-start(bf16[2,72,256]{2,1,0:T(8,128)(2,1)S(1)} %get-tuple-element.48), channel_id=1, source_target_pairs={{0,2},{1,3},{2,0},{3,1},{4,6},{5,7},{6,4},{7,5},{8,10},{9,11},{10,... | collective-permute-start | bytes 221192 | tf_op jit(solution)/shard_map/ppermute | solution.py:240
  47.4 0.4 collective-permute-start.8
  47.8 1.0 %collective-permute-start.11 = (f32[40,240]{1,0:T(8,128)S(1)}, f32[40,240]{1,0:T(8,128)S(1)}, u32[]{:S(2)}, u32[]{:S(2)}) collective-permute-start(f32[40,240]{1,0:T(8,128)S(1)} %add.91), channel_id=1, source_target_pairs={{0,16},{4,20},{8,24},{12,28},{16,0},{20,4},{24,8},{28,12},{1,17},{... | collective-permute-start | bytes 115208 | tf_op jit(solution)/shard_map/ppermute | solution.py:240
  48.8 4.1 %near.3.near_ref = f32[80,1024]{1,0:T(8,128)S(1)} custom-call(f32[1,8]{1,0:T(1,128)S(1)} %compare_select_fusion.flags, bf16[8,72,256]{2,1,0:T(8,128)(2,1)S(1)} %all-to-all-done.1.v_ref, bf16[1,8,2,1024,256]{4,3,2,1,0:T(8,128)(2,1)} %blocks_ref.3), custom_call_target="tpu_custom_call" | custom-call | tf_op jit(solution)/shard_map/near/pallas_call | solution.py:71
  53.0 0.3 collective-permute-done.11
  53.3 0.0 collective-permute-done.10
  53.3 0.0 collective-permute-done.9
  53.3 0.0 collective-permute-done.8
  53.4 0.6 far.3
  54.0 0.1 collective-permute-start.12
  54.1 1.4 %collective-permute-done.12 = f32[2,80,256]{2,1,0:T(8,128)S(1)} collective-permute-done((f32[2,80,256]{2,1,0:T(8,128)S(1)}, f32[2,80,256]{2,1,0:T(8,128)S(1)}, u32[]{:S(2)}, u32[]{:S(2)}) %collective-permute-start.12) | collective-permute-done | bytes 163872 | tf_op jit(solution)/shard_map/ppermute | solution.py:240
  55.5 1.2 %collective-permute-start.13 = (bf16[2,80,256]{2,1,0:T(8,128)(2,1)S(1)}, bf16[2,80,256]{2,1,0:T(8,128)(2,1)S(1)}, u32[]{:S(2)}, u32[]{:S(2)}) collective-permute-start(bf16[2,80,256]{2,1,0:T(8,128)(2,1)S(1)} %add_convert_fusion), channel_id=1, source_target_pairs={{0,2},{1,3},{2,0},{3,1},{4,6},{5,7},{6,4},{7,5},{8,10},{9,11},{10,... | collective-permute-start | bytes 245768 | tf_op jit(solution)/shard_map/ppermute | solution.py:240
  56.7 0.9 %collective-permute-start.15 = (f32[40,240]{1,0:T(8,128)S(1)}, f32[40,240]{1,0:T(8,128)S(1)}, u32[]{:S(2)}, u32[]{:S(2)}) collective-permute-start(f32[40,240]{1,0:T(8,128)S(1)} %add.92), channel_id=1, source_target_pairs={{0,8},{4,12},{8,0},{12,4},{16,24},{20,28},{24,16},{28,20},{1,9},{5... | collective-permute-start | bytes 115208 | tf_op jit(solution)/shard_map/ppermute | solution.py:240
  57.6 2.5 %collective-permute-done.13 = bf16[2,80,256]{2,1,0:T(8,128)(2,1)S(1)} collective-permute-done((bf16[2,80,256]{2,1,0:T(8,128)(2,1)S(1)}, bf16[2,80,256]{2,1,0:T(8,128)(2,1)S(1)}, u32[]{:S(2)}, u32[]{:S(2)}) %collective-permute-start.13) | collective-permute-done | bytes 81952 | tf_op jit(solution)/shard_map/ppermute | solution.py:240
  60.1 0.4 gram_two.1
  60.5 0.1 collective-permute-start.14
  60.5 0.5 collective-permute-start.17
  61.0 0.0 collective-permute-done.15
  61.1 0.7 collective-permute-done.14
  61.7 0.7 broadcast_in_dim.36
  62.4 3.9 %all-to-all-start.2 = ((f32[8,40,120]{2,1,0:T(8,128)}), f32[8,40,120]{2,1,0:T(8,128)S(1)}, u32[]{:S(2)}, u32[]{:S(2)}) async-start(f32[8,40,120]{2,1,0:T(8,128)} %broadcast_in_dim.36), calls=%async_computation.2 | async-start | bytes 327680 | tf_op jit(solution)/shard_map/all_to_all | solution.py:246
  66.4 2.0 %collective-permute-start.16 = (f32[40,240]{1,0:T(8,128)S(1)}, f32[40,240]{1,0:T(8,128)S(1)}, u32[]{:S(2)}, u32[]{:S(2)}) collective-permute-start(f32[40,240]{1,0:T(8,128)S(1)} %add.97), channel_id=1, source_target_pairs={{0,4},{4,0},{8,12},{12,8},{16,20},{20,16},{24,28},{28,24},{1,5},{5... | collective-permute-start | bytes 115208 | tf_op jit(solution)/shard_map/ppermute | solution.py:240
  68.4 0.0 collective-permute-done.17
  68.4 2.8 %collective-permute-done.16 = f32[40,240]{1,0:T(8,128)S(1)} collective-permute-done((f32[40,240]{1,0:T(8,128)S(1)}, f32[40,240]{1,0:T(8,128)S(1)}, u32[]{:S(2)}, u32[]{:S(2)}) %collective-permute-start.16) | collective-permute-done | bytes 38432 | tf_op jit(solution)/shard_map/ppermute | solution.py:240
  71.2 1.9 %invert.1.inv_ref = f32[40,80]{1,0:T(8,128)S(1)} custom-call(f32[40,240]{1,0:T(8,128)S(1)} %add.98.g1_ref), custom_call_target="tpu_custom_call" | custom-call | tf_op jit(solution)/shard_map/invert/pallas_call | solution.py:227
  73.2 1.0 %all-to-all-done.2.g2_ref = f32[8,40,120]{2,1,0:T(8,128)S(1)} async-done(((f32[8,40,120]{2,1,0:T(8,128)}), f32[8,40,120]{2,1,0:T(8,128)S(1)}, u32[]{:S(2)}, u32[]{:S(2)}) %all-to-all-start.2) | async-done | bytes 153632 | tf_op jit(solution)/shard_map/all_to_all | solution.py:246
  74.2 3.7 %solve.1 = (f32[36,2,1024]{2,1,0:T(2,128)}, f32[36,2,36]{2,1,0:T(2,128)}) custom-call(f32[40,80]{1,0:T(8,128)S(1)} %invert.1.inv_ref, f32[40,240]{1,0:T(8,128)S(1)} %add.98.g1_ref, f32[8,40,120]{2,1,0:T(8,128)S(1)} %all-to-all-done.2.g2_ref, f32[4,80,256]{2,1,0:T(8,128)S(1)} %pad_maximum_fusion.b_ref, f32[4,80,256]{2,1,0:T(8,128)S(1)} %bitcast.42), custom_call_target="tpu_custom_call" | custom-call | tf_op jit(solution)/shard_map/solve/pallas_call | solution.py:227
  (41 shorter events, 0.5 us)
Async XLA Ops:
  0.6 25.0 %copy-start.2 = (s32[1,8]{1,0:T(1,128)S(1)}, s32[1,8]{1,0:T(1,128)}, u32[]{:S(2)}) copy-start(s32[1,8]{1,0:T(1,128)} %flags.1) | copy-start | bytes 100
  0.6 25.0 %copy-start.3 = (s32[1,2]{1,0:T(1,128)S(1)}, s32[1,2]{1,0:T(1,128)}, u32[]{:S(2)}) copy-start(s32[1,2]{1,0:T(1,128)} %ranks.3) | copy-start | bytes 28
  0.7 25.0 %copy-start = (bf16[1,2,2,64,1024]{4,3,2,1,0:T(8,128)(2,1)S(1)}, bf16[1,2,2,64,1024]{4,3,2,1,0:T(8,128)(2,1)}, u32[]{:S(2)}) copy-start(bf16[1,2,2,64,1024]{4,3,2,1,0:T(8,128)(2,1)} %param.12) | copy-start | bytes 1572868
  0.7 25.0 %copy-start.1 = (bf16[1,2,2,64,1024]{4,3,2,1,0:T(8,128)(2,1)S(1)}, bf16[1,2,2,64,1024]{4,3,2,1,0:T(8,128)(2,1)}, u32[]{:S(2)}) copy-start(bf16[1,2,2,64,1024]{4,3,2,1,0:T(8,128)(2,1)} %param.11) | copy-start | bytes 1572868
  2.5 16.9 %all-to-all-start = ((bf16[8,72,256]{2,1,0:T(8,128)(2,1)}), bf16[8,72,256]{2,1,0:T(8,128)(2,1)S(1)}, u32[]{:S(2)}, u32[]{:S(2)}) async-start(bf16[8,72,256]{2,1,0:T(8,128)(2,1)} %broadcast_in_dim.16), calls=%async_computation | async-start | bytes 589824 | tf_op jit(solution)/shard_map/all_to_all | solution.py:281
  19.4 6.1 %collective-permute-start.2 = (bf16[2,72,256]{2,1,0:T(8,128)(2,1)S(1)}, bf16[2,72,256]{2,1,0:T(8,128)(2,1)S(1)}, u32[]{:S(2)}, u32[]{:S(2)}) collective-permute-start(bf16[2,72,256]{2,1,0:T(8,128)(2,1)S(1)} %get-tuple-element.51), channel_id=1, source_target_pairs={{0,3},{1,2},{2,1},{3,0},{4,7},{5,6},{6,5},{7,4},{8,11},{9,10},{10,... | collective-permute-start | bytes 221192 | tf_op jit(solution)/shard_map/ppermute | solution.py:240
  19.4 6.1 %collective-permute-start.1 = (bf16[2,72,256]{2,1,0:T(8,128)(2,1)S(1)}, bf16[2,72,256]{2,1,0:T(8,128)(2,1)S(1)}, u32[]{:S(2)}, u32[]{:S(2)}) collective-permute-start(bf16[2,72,256]{2,1,0:T(8,128)(2,1)S(1)} %get-tuple-element.52), channel_id=1, source_target_pairs={{0,2},{1,3},{2,0},{3,1},{4,6},{5,7},{6,4},{7,5},{8,10},{9,11},{10,... | collective-permute-start | bytes 221192 | tf_op jit(solution)/shard_map/ppermute | solution.py:240
  21.0 4.6 %collective-permute-start = (bf16[2,72,256]{2,1,0:T(8,128)(2,1)S(1)}, bf16[2,72,256]{2,1,0:T(8,128)(2,1)S(1)}, u32[]{:S(2)}, u32[]{:S(2)}) collective-permute-start(bf16[2,72,256]{2,1,0:T(8,128)(2,1)S(1)} %get-tuple-element.53), channel_id=1, source_target_pairs={{0,1},{1,0},{2,3},{3,2},{4,5},{5,4},{6,7},{7,6},{8,9},{9,8},{10,11... | collective-permute-start | bytes 221192 | tf_op jit(solution)/shard_map/ppermute | solution.py:240
  26.3 1.5 %collective-permute-start.3 = (f32[2,80,256]{2,1,0:T(8,128)S(1)}, f32[2,80,256]{2,1,0:T(8,128)S(1)}, u32[]{:S(2)}, u32[]{:S(2)}) collective-permute-start(f32[2,80,256]{2,1,0:T(8,128)S(1)} %slice.46), channel_id=1, source_target_pairs={{0,1},{1,0},{2,3},{3,2},{4,5},{5,4},{6,7},{7,6},{8,9},{9,8},{10,11... | collective-permute-start | bytes 491528 | tf_op jit(solution)/shard_map/ppermute | solution.py:240
  27.8 4.6 %collective-permute-start.4 = (f32[1,80,256]{2,1,0:T(8,128)S(1)}, f32[1,80,256]{2,1,0:T(8,128)S(1)}, u32[]{:S(2)}, u32[]{:S(2)}) collective-permute-start(f32[1,80,256]{2,1,0:T(8,128)S(1)} %slice.59), channel_id=1, source_target_pairs={{0,2},{1,3},{2,0},{3,1},{4,6},{5,7},{6,4},{7,5},{8,10},{9,11},{10,... | collective-permute-start | bytes 245768 | tf_op jit(solution)/shard_map/ppermute | solution.py:240
  33.2 12.7 %all-to-all-start.1 = ((bf16[8,72,256]{2,1,0:T(8,128)(2,1)}), bf16[8,72,256]{2,1,0:T(8,128)(2,1)S(1)}, u32[]{:S(2)}, u32[]{:S(2)}) async-start(bf16[8,72,256]{2,1,0:T(8,128)(2,1)} %broadcast_in_dim.34), calls=%async_computation.1 | async-start | bytes 589824 | tf_op jit(solution)/shard_map/all_to_all | solution.py:326
  36.8 7.1 %collective-permute-start.7 = (f32[1,80,256]{2,1,0:T(8,128)S(1)}, f32[1,80,256]{2,1,0:T(8,128)S(1)}, u32[]{:S(2)}, u32[]{:S(2)}) collective-permute-start(f32[1,80,256]{2,1,0:T(8,128)S(1)} %bitcast.43), channel_id=1, source_target_pairs={{0,2},{1,3},{2,0},{3,1},{4,6},{5,7},{6,4},{7,5},{8,10},{9,11},{10,... | collective-permute-start | bytes 245768 | tf_op jit(solution)/shard_map/ppermute | solution.py:240
  38.6 1.3 %collective-permute-start.5 = (f32[40,240]{1,0:T(8,128)S(1)}, f32[40,240]{1,0:T(8,128)S(1)}, u32[]{:S(2)}, u32[]{:S(2)}) collective-permute-start(f32[40,240]{1,0:T(8,128)S(1)} %gram_one.1), channel_id=1, source_target_pairs={{0,1},{1,0},{2,3},{3,2},{4,5},{5,4},{6,7},{7,6},{8,9},{9,8},{10,11... | collective-permute-start | bytes 115208 | tf_op jit(solution)/shard_map/ppermute | solution.py:240
  39.9 4.0 %collective-permute-start.6 = (f32[40,240]{1,0:T(8,128)S(1)}, f32[40,240]{1,0:T(8,128)S(1)}, u32[]{:S(2)}, u32[]{:S(2)}) collective-permute-start(f32[40,240]{1,0:T(8,128)S(1)} %add.90), channel_id=1, source_target_pairs={{0,2},{1,3},{2,0},{3,1},{4,6},{5,7},{6,4},{7,5},{8,10},{9,11},{10,... | collective-permute-start | bytes 115208 | tf_op jit(solution)/shard_map/ppermute | solution.py:240
  45.9 7.4 %collective-permute-start.10 = (bf16[2,72,256]{2,1,0:T(8,128)(2,1)S(1)}, bf16[2,72,256]{2,1,0:T(8,128)(2,1)S(1)}, u32[]{:S(2)}, u32[]{:S(2)}) collective-permute-start(bf16[2,72,256]{2,1,0:T(8,128)(2,1)S(1)} %get-tuple-element.47), channel_id=1, source_target_pairs={{0,3},{1,2},{2,1},{3,0},{4,7},{5,6},{6,5},{7,4},{8,11},{9,10},{10,... | collective-permute-start | bytes 221192 | tf_op jit(solution)/shard_map/ppermute | solution.py:240
  45.9 7.3 %collective-permute-start.9 = (bf16[2,72,256]{2,1,0:T(8,128)(2,1)S(1)}, bf16[2,72,256]{2,1,0:T(8,128)(2,1)S(1)}, u32[]{:S(2)}, u32[]{:S(2)}) collective-permute-start(bf16[2,72,256]{2,1,0:T(8,128)(2,1)S(1)} %get-tuple-element.48), channel_id=1, source_target_pairs={{0,2},{1,3},{2,0},{3,1},{4,6},{5,7},{6,4},{7,5},{8,10},{9,11},{10,... | collective-permute-start | bytes 221192 | tf_op jit(solution)/shard_map/ppermute | solution.py:240
  47.4 5.9 %collective-permute-start.8 = (bf16[2,72,256]{2,1,0:T(8,128)(2,1)S(1)}, bf16[2,72,256]{2,1,0:T(8,128)(2,1)S(1)}, u32[]{:S(2)}, u32[]{:S(2)}) collective-permute-start(bf16[2,72,256]{2,1,0:T(8,128)(2,1)S(1)} %get-tuple-element.49), channel_id=1, source_target_pairs={{0,1},{1,0},{2,3},{3,2},{4,5},{5,4},{6,7},{7,6},{8,9},{9,8},{10,11... | collective-permute-start | bytes 221192 | tf_op jit(solution)/shard_map/ppermute | solution.py:240
  47.8 5.5 %collective-permute-start.11 = (f32[40,240]{1,0:T(8,128)S(1)}, f32[40,240]{1,0:T(8,128)S(1)}, u32[]{:S(2)}, u32[]{:S(2)}) collective-permute-start(f32[40,240]{1,0:T(8,128)S(1)} %add.91), channel_id=1, source_target_pairs={{0,16},{4,20},{8,24},{12,28},{16,0},{20,4},{24,8},{28,12},{1,17},{... | collective-permute-start | bytes 115208 | tf_op jit(solution)/shard_map/ppermute | solution.py:240
  54.0 1.5 %collective-permute-start.12 = (f32[2,80,256]{2,1,0:T(8,128)S(1)}, f32[2,80,256]{2,1,0:T(8,128)S(1)}, u32[]{:S(2)}, u32[]{:S(2)}) collective-permute-start(f32[2,80,256]{2,1,0:T(8,128)S(1)} %slice.53), channel_id=1, source_target_pairs={{0,1},{1,0},{2,3},{3,2},{4,5},{5,4},{6,7},{7,6},{8,9},{9,8},{10,11... | collective-permute-start | bytes 491528 | tf_op jit(solution)/shard_map/ppermute | solution.py:240
  55.5 4.6 %collective-permute-start.13 = (bf16[2,80,256]{2,1,0:T(8,128)(2,1)S(1)}, bf16[2,80,256]{2,1,0:T(8,128)(2,1)S(1)}, u32[]{:S(2)}, u32[]{:S(2)}) collective-permute-start(bf16[2,80,256]{2,1,0:T(8,128)(2,1)S(1)} %add_convert_fusion), channel_id=1, source_target_pairs={{0,2},{1,3},{2,0},{3,1},{4,6},{5,7},{6,4},{7,5},{8,10},{9,11},{10,... | collective-permute-start | bytes 245768 | tf_op jit(solution)/shard_map/ppermute | solution.py:240
  56.7 4.4 %collective-permute-start.15 = (f32[40,240]{1,0:T(8,128)S(1)}, f32[40,240]{1,0:T(8,128)S(1)}, u32[]{:S(2)}, u32[]{:S(2)}) collective-permute-start(f32[40,240]{1,0:T(8,128)S(1)} %add.92), channel_id=1, source_target_pairs={{0,8},{4,12},{8,0},{12,4},{16,24},{20,28},{24,16},{28,20},{1,9},{5... | collective-permute-start | bytes 115208 | tf_op jit(solution)/shard_map/ppermute | solution.py:240
  60.5 1.2 %collective-permute-start.14 = (f32[40,120]{1,0:T(8,128)S(1)}, f32[40,120]{1,0:T(8,128)S(1)}, u32[]{:S(2)}, u32[]{:S(2)}) collective-permute-start(f32[40,120]{1,0:T(8,128)S(1)} %gram_two.1), channel_id=1, source_target_pairs={{0,1},{1,0},{2,3},{3,2},{4,5},{5,4},{6,7},{7,6},{8,9},{9,8},{10,11... | collective-permute-start | bytes 57608 | tf_op jit(solution)/shard_map/ppermute | solution.py:240
  60.5 7.8 %collective-permute-start.17 = (f32[2,80,256]{2,1,0:T(8,128)S(1)}, f32[2,80,256]{2,1,0:T(8,128)S(1)}, u32[]{:S(2)}, u32[]{:S(2)}) collective-permute-start(f32[2,80,256]{2,1,0:T(8,128)S(1)} %pad_maximum_fusion.4.p_ref), channel_id=1, source_target_pairs={{0,1},{1,0},{2,3},{3,2},{4,5},{5,4},{6,7},{7,6},{8,9},{9,8},{10,11... | collective-permute-start | bytes 491528 | tf_op jit(solution)/shard_map/ppermute | solution.py:240
  62.4 11.7 %all-to-all-start.2 = ((f32[8,40,120]{2,1,0:T(8,128)}), f32[8,40,120]{2,1,0:T(8,128)S(1)}, u32[]{:S(2)}, u32[]{:S(2)}) async-start(f32[8,40,120]{2,1,0:T(8,128)} %broadcast_in_dim.36), calls=%async_computation.2 | async-start | bytes 327680 | tf_op jit(solution)/shard_map/all_to_all | solution.py:246
  66.4 4.9 %collective-permute-start.16 = (f32[40,240]{1,0:T(8,128)S(1)}, f32[40,240]{1,0:T(8,128)S(1)}, u32[]{:S(2)}, u32[]{:S(2)}) collective-permute-start(f32[40,240]{1,0:T(8,128)S(1)} %add.97), channel_id=1, source_target_pairs={{0,4},{4,0},{8,12},{12,8},{16,20},{20,16},{24,28},{28,24},{1,5},{5... | collective-permute-start | bytes 115208 | tf_op jit(solution)/shard_map/ppermute | solution.py:240
